TPU v7x, 32 devices: a whole 2x2x4 slice. The times are simulated.
32 devices in a mesh: region: 8 (over z, x), mp: 4 (over y, core).
Axes of the slice: x: 2, y: 2, z: 4, core: 2. Of those that a mesh axis runs over, the one named last changes fastest.
Arguments:
- tile_data: bfloat16 [32, 256, 2048], P('region', None, 'mp'), may hold values from -6.5 to 6.5
- tile_counts: int32 [8], replicated, may hold values from 0 to 4, as said below
- modulation: bfloat16 [8, 3, 2048], P('region'), may hold values from -4 to 4
- qkv_weight: bfloat16 [2048, 3, 2048], P('region', None, 'mp'), may hold values from -0.92807765 to 0.92807765
- out_weight: bfloat16 [2048, 2048], P('region', 'mp'), may hold values from -0.125 to 0.125
- blend_weights: float32 [6], replicated, may hold values from 0.1 to 0.9
Outputs:
- blended: bfloat16 [32, 256, 2048], P('region', None, 'mp')
Inputs may be any that keep to these rules, and one draw needn't show every extreme that they name: `tile_counts`: groups 2m and 2m + 1 together hold exactly 4 tiles. In every draw some group holds 4 tiles and its partner none.
All inputs are finite; a program needn't handle non-finite values.
Results may differ from a plain program's by a relative error of at most 0.0071.
Values may be sent and summed in bfloat16 or wider, within the bound.
A program may use at most 64 MiB of HBM per device.

v0:
```python
import math

import jax
import jax.numpy as jnp
from jax import lax
from jax.sharding import PartitionSpec as P

D = 2048
HDIM = 128
S = 16
W = 6
TCOLS = 8
TPD = 2


def from_behind(block, axis, distance):
    devices = range(lax.axis_size(axis))
    route = [(i - distance, i) for i in devices if i - distance in devices]
    return lax.ppermute(block, axis, route)


def normalise(values):
    row_mean = jnp.mean(values, axis=-1, keepdims=True)
    centred = values - row_mean
    spread = jnp.mean(centred * centred, axis=-1, keepdims=True)
    return centred * lax.rsqrt(spread + 1e-06)


def attend(local_rows, modulators, qkv_weight, out_weight):
    tile_count = local_rows.shape[0]
    tokens = local_rows.shape[1]
    narrow = local_rows.shape[2]
    gathered = lax.all_gather(local_rows, "mp", axis=2, tiled=True)
    mod_values = modulators.astype(jnp.float32)
    hidden = (
        normalise(gathered.astype(jnp.float32)) * (1.0 + mod_values[:, 1][:, None, :])
        + mod_values[:, 0][:, None, :]
    )
    hidden = hidden.astype(jnp.bfloat16).reshape(tile_count * tokens, D)
    weight_piece = lax.all_gather(qkv_weight, "region", axis=0, tiled=True)
    flat_piece = weight_piece.reshape(weight_piece.shape[0], 3 * narrow)
    projections = jnp.dot(hidden, flat_piece, preferred_element_type=jnp.float32).astype(
        jnp.bfloat16
    )
    projections = projections.reshape(tile_count, tokens, 3, narrow // HDIM, HDIM)
    scores = jnp.einsum(
        "nqhe,nkhe->nhqk",
        projections[:, :, 0],
        projections[:, :, 1],
        preferred_element_type=jnp.float32,
    )
    scores = scores / math.sqrt(HDIM)
    attention_weights = jax.nn.softmax(scores, axis=-1).astype(jnp.bfloat16)
    attended = jnp.einsum(
        "nhqk,nkhe->nqhe",
        attention_weights,
        projections[:, :, 2],
        preferred_element_type=jnp.float32,
    )
    attended = attended.astype(jnp.bfloat16).reshape(tile_count * tokens, narrow)
    partial_out = jnp.einsum(
        "rd,md->rm",
        attended,
        lax.all_gather(out_weight, "region", axis=0, tiled=True),
        preferred_element_type=jnp.float32,
    )
    summed = lax.psum_scatter(partial_out, "mp", scatter_dimension=1, tiled=True)
    gate_slice = lax.dynamic_slice_in_dim(
        mod_values[:, 2], lax.axis_index("mp") * narrow, narrow, 1
    )
    updated = local_rows.astype(jnp.float32) + gate_slice[:, None, :] * summed.reshape(
        tile_count, tokens, narrow
    )
    return updated.astype(jnp.bfloat16)


def join_edges(tile_grid, earlier_rim, later_rim, has_before, has_after, shares, edge_axis):
    rim_width = shares.shape[0]
    side_len = tile_grid.shape[edge_axis]
    share_shape = [1, 1, 1, 1]
    share_shape[edge_axis] = rim_width
    share_view = shares.reshape(share_shape)
    near_part = lax.slice_in_dim(tile_grid, 0, rim_width, axis=edge_axis)
    middle = lax.slice_in_dim(tile_grid, rim_width, side_len - rim_width, axis=edge_axis)
    far_part = lax.slice_in_dim(tile_grid, side_len - rim_width, side_len, axis=edge_axis)
    near_mix = (1.0 - share_view) * earlier_rim + share_view * near_part
    far_mix = (1.0 - share_view) * far_part + share_view * later_rim
    near_part = jnp.where(has_before[:, None, None, None], near_mix, near_part)
    far_part = jnp.where(has_after[:, None, None, None], far_mix, far_part)
    return jnp.concatenate([near_part, middle, far_part], axis=edge_axis)


def locate(targets, tile_counts, slot_count):
    pair_of = targets // slot_count
    within = targets - pair_of * slot_count
    group_ids = jnp.arange(tile_counts.shape[0], dtype=jnp.int32)
    even_of = jnp.sum(
        jnp.where(group_ids[None, :] == 2 * pair_of[:, None], tile_counts[None, :], 0), axis=1
    )
    in_second = (within >= even_of).astype(jnp.int32)
    return (2 * pair_of + in_second, within - in_second * even_of)


def on_device(tile_data, tile_counts, modulation, qkv_weight, out_weight, blend_weights):
    device_id = lax.axis_index("region")
    parity_bit = device_id % 2
    pair_base = device_id - parity_bit
    group_ids = jnp.arange(tile_counts.shape[0], dtype=jnp.int32)
    even_count = jnp.sum(jnp.where(group_ids == pair_base, tile_counts, 0))
    own_count = jnp.sum(jnp.where(group_ids == device_id, tile_counts, 0))
    tile_total = TPD * tile_counts.shape[0]
    slot_count = tile_data.shape[0]
    narrow = tile_data.shape[2]
    slot_ids = jnp.arange(slot_count, dtype=jnp.int32)
    live_slots = slot_ids < own_count
    modulators = jnp.broadcast_to(modulation, (slot_count, 3, D))
    updated = attend(tile_data, modulators, qkv_weight, out_weight)
    tile_grid = updated.reshape(slot_count, S, S, narrow)
    tile_ids = device_id // 2 * slot_count + parity_bit * even_count + slot_ids
    column_pos = tile_ids % TCOLS
    has_left = live_slots & (column_pos != 0)
    has_right = live_slots & (column_pos != TCOLS - 1)
    right_device, right_slot = locate(tile_ids + 1, tile_counts, slot_count)
    left_device, left_slot = locate(tile_ids - 1, tile_counts, slot_count)
    west_edge = tile_grid[:, :, :W]
    east_edge = tile_grid[:, :, S - W :]
    later_stack = jnp.concatenate(
        [west_edge]
        + [from_behind(west_edge, "region", -offset_step) for offset_step in range(1, 4)],
        axis=0,
    )
    pick_index = jnp.clip(
        (right_device - device_id) * slot_count + right_slot, 0, 4 * slot_count - 1
    )
    later_rim = jnp.take(later_stack, pick_index, axis=0).astype(jnp.float32)
    earlier_stack = jnp.concatenate(
        [east_edge]
        + [from_behind(east_edge, "region", offset_step) for offset_step in range(1, 4)],
        axis=0,
    )
    pick_index = jnp.clip((device_id - left_device) * slot_count + left_slot, 0, 4 * slot_count - 1)
    earlier_rim = jnp.take(earlier_stack, pick_index, axis=0).astype(jnp.float32)
    joined = join_edges(
        tile_grid.astype(jnp.float32), earlier_rim, later_rim, has_left, has_right, blend_weights, 2
    )
    joined = joined.astype(jnp.bfloat16)
    lowest = max(0, 2 * (TCOLS // slot_count) - 1)
    highest = 2 * -(-TCOLS // slot_count) + 1
    offsets = list(range(lowest, highest + 1))
    north_edge = joined[:, :W]
    south_edge = joined[:, S - W :]
    below_device, below_slot = locate(tile_ids + TCOLS, tile_counts, slot_count)
    above_device, above_slot = locate(tile_ids - TCOLS, tile_counts, slot_count)
    has_below = live_slots & (tile_ids + TCOLS < tile_total)
    has_above = live_slots & (tile_ids >= TCOLS)
    rising = [from_behind(north_edge, "region", -offset_step) for offset_step in offsets]
    later_stack = jnp.concatenate(rising, axis=0)
    pick_index = jnp.clip(
        (below_device - device_id - lowest) * slot_count + below_slot,
        0,
        len(offsets) * slot_count - 1,
    )
    later_rim = jnp.take(later_stack, pick_index, axis=0).astype(jnp.float32)
    falling = [from_behind(south_edge, "region", offset_step) for offset_step in offsets]
    earlier_stack = jnp.concatenate(falling, axis=0)
    pick_index = jnp.clip(
        (device_id - above_device - lowest) * slot_count + above_slot,
        0,
        len(offsets) * slot_count - 1,
    )
    earlier_rim = jnp.take(earlier_stack, pick_index, axis=0).astype(jnp.float32)
    finished = join_edges(
        joined.astype(jnp.float32), earlier_rim, later_rim, has_above, has_below, blend_weights, 1
    )
    finished = jnp.where(live_slots[:, None, None, None], finished, 0.0)
    result = finished.astype(jnp.bfloat16).reshape(slot_count, S * S, narrow)
    return result


def solution(mesh):
    return jax.shard_map(
        on_device,
        mesh=mesh,
        in_specs=(
            P("region", None, "mp"),
            P(),
            P("region", None, None),
            P("region", None, "mp"),
            P("region", "mp"),
            P(),
        ),
        out_specs=P("region", None, "mp"),
        check_vma=False,
    )
```

profile of v0, /device:TPU:27, one launch (start us, length us, event | category | flops | bytes accessed | tf_op | source)
XLA Modules:
  0.0 404.9 jit_solution(10843375741006684771)
XLA Ops:
  7.3 2.3 copy.17
  10.5 34.3 %all-gather.4.cloned.1.call-done = bf16[4,256,2048]{2,1,0:T(8,128)(2,1)} async-done(((bf16[4,256,512]{2,1,0:T(8,128)(2,1)}), bf16[4,256,2048]{2,1,0:T(8,128)(2,1)}) %all-gather.4.cloned.1.call-update) | async-done | bytes 4194320 | tf_op jit(solution)/shard_map/all_gather | solution.py:33
  44.8 3.0 convert_reduce_fusion
  49.5 3.1 fusion.6
  52.6 91.2 %all-gather.6.cloned.1.call-done = bf16[2048,3,512]{0,2,1:T(8,128)(2,1)} async-done(((bf16[256,3,512]{0,2,1:T(8,128)(2,1)}), bf16[2048,3,512]{0,2,1:T(8,128)(2,1)}) %all-gather.6.cloned.1.call-update) | async-done | bytes 6291472 | tf_op jit(solution)/shard_map/all_gather | solution.py:40
  143.8 11.3 %convolution_convert_fusion = bf16[1024,1536]{1,0:T(8,128)(2,1)} fusion(bf16[1024,2048]{1,0:T(8,128)(2,1)} %bitcast.33, bf16[2048,1536]{0,1:T(8,128)(2,1)} %bitcast.39), kind=kOutput, calls=%fused_computation.15 | convolution fusion | flops 6444023808 | bytes 13631488 | tf_op jit(solution)/shard_map/dot_general | solution.py:42
  155.0 5.0 %reshape.199 = bf16[4,256,3,4,128]{4,3,2,1,0:T(4,128)(2,1)S(1)} reshape(bf16[1024,1536]{1,0:T(8,128)(2,1)} %convolution_convert_fusion) | data formatting | bytes 6291456 | tf_op jit(solution)/shard_map/reshape | solution.py:45
  160.0 2.5 fusion.45
  165.1 3.2 fusion.49
  169.5 24.0 %all-gather.8.cloned.1.call-done = bf16[2048,512]{1,0:T(8,128)(2,1)} async-done(((bf16[256,512]{1,0:T(8,128)(2,1)}), bf16[2048,512]{1,0:T(8,128)(2,1)}) %all-gather.8.cloned.1.call-update) | async-done | bytes 2097168 | tf_op jit(solution)/shard_map/all_gather | solution.py:64
  193.5 7.2 %fusion.15 = f32[1024,2048]{1,0:T(8,128)} fusion(bf16[2048,512]{1,0:T(8,128)(2,1)} %all-gather.8.cloned.1.call-done, bf16[128,8,4,128]{3,2,1,0:T(4,128)(2,1)S(1)} %bitcast.35), kind=kOutput, calls=%fused_computation.30 | convolution fusion | flops 2147483648 | bytes 11534336 | tf_op jit(solution)/shard_map/rd,md->rm/dot_general | solution.py:61
  203.0 70.6 %reduce-scatter.2.cloned.1.call-done = f32[1024,512]{1,0:T(8,128)} async-done(((f32[1024,2048]{1,0:T(8,128)}), f32[1024,512]{1,0:T(8,128)}) %reduce-scatter.2.cloned.1.call-update) | async-done | bytes 2097168 | tf_op jit(solution)/shard_map/reduce_scatter | solution.py:67
  275.7 2.4 collective-permute-start.3
  280.3 3.0 collective-permute-start.5
  286.7 11.4 %collective-permute-done.3 = bf16[4,16,6,512]{3,2,1,0:T(8,128)(2,1)S(1)} collective-permute-done((bf16[4,16,6,512]{3,2,1,0:T(8,128)(2,1)S(1)}, bf16[4,16,6,512]{3,2,1,0:T(8,128)(2,1)S(1)}, u32[]{:S(2)}, u32[]{:S(2)}) %collective-permute-start.3) | collective-permute-done | bytes 393248 | tf_op jit(solution)/shard_map/ppermute | solution.py:19
  299.9 7.6 %collective-permute-done.5 = bf16[4,16,6,512]{3,2,1,0:T(8,128)(2,1)S(1)} collective-permute-done((bf16[4,16,6,512]{3,2,1,0:T(8,128)(2,1)S(1)}, bf16[4,16,6,512]{3,2,1,0:T(8,128)(2,1)S(1)}, u32[]{:S(2)}, u32[]{:S(2)}) %collective-permute-start.5) | collective-permute-done | bytes 393248 | tf_op jit(solution)/shard_map/ppermute | solution.py:19
  309.3 2.2 gather_fusion.1
  311.5 14.3 %collective-permute-done.2 = bf16[4,16,6,512]{3,2,1,0:T(8,128)(2,1)} collective-permute-done((bf16[4,16,6,512]{3,2,1,0:T(8,128)(2,1)S(1)}, bf16[4,16,6,512]{3,2,1,0:T(8,128)(2,1)}, u32[]{:S(2)}, u32[]{:S(2)}) %collective-permute-start.2) | collective-permute-done | bytes 393248 | tf_op jit(solution)/shard_map/ppermute | solution.py:19
  325.8 3.2 pad_maximum_fusion
  329.0 2.2 gather_fusion
  333.2 11.1 %collective-permute-start.10 = (bf16[4,6,16,512]{3,2,1,0:T(8,128)(2,1)S(1)}, bf16[4,6,16,512]{3,2,1,0:T(8,128)(2,1)S(1)}, u32[]{:S(2)}, u32[]{:S(2)}) collective-permute-start(bf16[4,6,16,512]{3,2,1,0:T(8,128)(2,1)S(1)} %get-tuple-element.31), channel_id=1, source_target_pairs={{16,0},{20,4},{24,8},{28,12},{17,1},{21,5},{25,9},{29,13},{18,2},{... | collective-permute-start | bytes 1179656 | tf_op jit(solution)/shard_map/ppermute | solution.py:19
  353.9 5.5 %collective-permute-done.11 = bf16[4,6,16,512]{3,2,1,0:T(8,128)(2,1)S(1)} collective-permute-done((bf16[4,6,16,512]{3,2,1,0:T(8,128)(2,1)S(1)}, bf16[4,6,16,512]{3,2,1,0:T(8,128)(2,1)S(1)}, u32[]{:S(2)}, u32[]{:S(2)}) %collective-permute-start.11) | collective-permute-done | bytes 393248 | tf_op jit(solution)/shard_map/ppermute | solution.py:19
  359.4 8.4 %collective-permute-done.9 = bf16[4,6,16,512]{3,2,1,0:T(8,128)(2,1)S(1)} collective-permute-done((bf16[4,6,16,512]{3,2,1,0:T(8,128)(2,1)S(1)}, bf16[4,6,16,512]{3,2,1,0:T(8,128)(2,1)S(1)}, u32[]{:S(2)}, u32[]{:S(2)}) %collective-permute-start.9) | collective-permute-done | bytes 393248 | tf_op jit(solution)/shard_map/ppermute | solution.py:19
  369.3 23.3 %collective-permute-done.7 = bf16[4,6,16,512]{3,2,1,0:T(8,128)(2,1)} collective-permute-done((bf16[4,6,16,512]{3,2,1,0:T(8,128)(2,1)}, bf16[4,6,16,512]{3,2,1,0:T(8,128)(2,1)}, u32[]{:S(2)}, u32[]{:S(2)}) %collective-permute-start.7) | collective-permute-done | bytes 393248 | tf_op jit(solution)/shard_map/ppermute | solution.py:19
  (84 shorter events, 38.3 us)
Async XLA Ops:
  6.5 3.9 copy-start.4
  6.5 38.3 %all-gather.4.cloned.1.call-start = ((), (), s32[]{:S(2)}) async-start(), calls=%async_computation.1 | async-start | bytes 5242880 | tf_op jit(solution)/shard_map/all_gather | solution.py:33
  7.3 136.5 %all-gather.6.cloned.1.call-start = ((), (), s32[]{:S(2)}) async-start(), calls=%async_computation.2 | async-start | bytes 7077888 | tf_op jit(solution)/shard_map/all_gather | solution.py:40
  9.6 183.9 %all-gather.8.cloned.1.call-start = ((), (), s32[]{:S(2)}) async-start(), calls=%async_computation.3 | async-start | bytes 2359296 | tf_op jit(solution)/shard_map/all_gather | solution.py:64
  10.4 263.3 %reduce-scatter.2.cloned.1.call-start = ((), (), s32[]{:S(2)}) async-start(), calls=%async_computation.4 | async-start | bytes 10485760 | tf_op jit(solution)/shard_map/reduce_scatter | solution.py:67
  44.8 3.4 copy-start
  162.5 1.7 copy-start.2
  162.5 1.9 copy-start.3
  200.7 72.9 %copy-start.1 = (bf16[4,256,512]{2,1,0:T(8,128)(2,1)S(1)}, bf16[4,256,512]{2,1,0:T(8,128)(2,1)}, u32[]{:S(2)}) copy-start(bf16[4,256,512]{2,1,0:T(8,128)(2,1)} %param.10) | copy-start | bytes 3145732
  275.6 23.8 %copy-start.5 = (f32[6]{0:T(128)S(1)}, f32[6]{0:T(128)}, u32[]{:S(2)}) copy-start(f32[6]{0:T(128)} %param.15) | copy-start | bytes 76
  275.7 22.4 %collective-permute-start.3 = (bf16[4,16,6,512]{3,2,1,0:T(8,128)(2,1)S(1)}, bf16[4,16,6,512]{3,2,1,0:T(8,128)(2,1)S(1)}, u32[]{:S(2)}, u32[]{:S(2)}) collective-permute-start(bf16[4,16,6,512]{3,2,1,0:T(8,128)(2,1)S(1)} %get-tuple-element.33), channel_id=1, source_target_pairs={{4,0},{8,4},{12,8},{16,12},{20,16},{24,20},{28,24},{5,1},{9,5},{13... | collective-permute-start | bytes 1179656 | tf_op jit(solution)/shard_map/ppermute | solution.py:19
  278.2 21.7 %collective-permute-start.4 = (bf16[4,16,6,512]{3,2,1,0:T(8,128)(2,1)S(1)}, bf16[4,16,6,512]{3,2,1,0:T(8,128)(2,1)S(1)}, u32[]{:S(2)}, u32[]{:S(2)}) collective-permute-start(bf16[4,16,6,512]{3,2,1,0:T(8,128)(2,1)S(1)} %get-tuple-element.33), channel_id=1, source_target_pairs={{8,0},{12,4},{16,8},{20,12},{24,16},{28,20},{9,1},{13,5},{17,9},{2... | collective-permute-start | bytes 1179656 | tf_op jit(solution)/shard_map/ppermute | solution.py:19
  280.3 27.1 %collective-permute-start.5 = (bf16[4,16,6,512]{3,2,1,0:T(8,128)(2,1)S(1)}, bf16[4,16,6,512]{3,2,1,0:T(8,128)(2,1)S(1)}, u32[]{:S(2)}, u32[]{:S(2)}) collective-permute-start(bf16[4,16,6,512]{3,2,1,0:T(8,128)(2,1)S(1)} %get-tuple-element.33), channel_id=1, source_target_pairs={{12,0},{16,4},{20,8},{24,12},{28,16},{13,1},{17,5},{21,9},{25,13},... | collective-permute-start | bytes 1179656 | tf_op jit(solution)/shard_map/ppermute | solution.py:19
  284.1 27.5 %collective-permute-start = (bf16[4,16,6,512]{3,2,1,0:T(8,128)(2,1)S(1)}, bf16[4,16,6,512]{3,2,1,0:T(8,128)(2,1)}, u32[]{:S(2)}, u32[]{:S(2)}) collective-permute-start(bf16[4,16,6,512]{3,2,1,0:T(8,128)(2,1)S(1)} %get-tuple-element.32), channel_id=1, source_target_pairs={{0,4},{4,8},{8,12},{12,16},{16,20},{20,24},{24,28},{1,5},{5,9},{9,... | collective-permute-start | bytes 1179656 | tf_op jit(solution)/shard_map/ppermute | solution.py:19
  285.4 26.2 %collective-permute-start.1 = (bf16[4,16,6,512]{3,2,1,0:T(8,128)(2,1)S(1)}, bf16[4,16,6,512]{3,2,1,0:T(8,128)(2,1)}, u32[]{:S(2)}, u32[]{:S(2)}) collective-permute-start(bf16[4,16,6,512]{3,2,1,0:T(8,128)(2,1)S(1)} %get-tuple-element.32), channel_id=1, source_target_pairs={{0,8},{4,12},{8,16},{12,20},{16,24},{20,28},{1,9},{5,13},{9,17},{1... | collective-permute-start | bytes 1179656 | tf_op jit(solution)/shard_map/ppermute | solution.py:19
  298.1 27.7 %collective-permute-start.2 = (bf16[4,16,6,512]{3,2,1,0:T(8,128)(2,1)S(1)}, bf16[4,16,6,512]{3,2,1,0:T(8,128)(2,1)}, u32[]{:S(2)}, u32[]{:S(2)}) collective-permute-start(bf16[4,16,6,512]{3,2,1,0:T(8,128)(2,1)S(1)} %get-tuple-element.32), channel_id=1, source_target_pairs={{0,12},{4,16},{8,20},{12,24},{16,28},{1,13},{5,17},{9,21},{13,25},... | collective-permute-start | bytes 1179656 | tf_op jit(solution)/shard_map/ppermute | solution.py:19
  333.2 18.2 %collective-permute-start.10 = (bf16[4,6,16,512]{3,2,1,0:T(8,128)(2,1)S(1)}, bf16[4,6,16,512]{3,2,1,0:T(8,128)(2,1)S(1)}, u32[]{:S(2)}, u32[]{:S(2)}) collective-permute-start(bf16[4,6,16,512]{3,2,1,0:T(8,128)(2,1)S(1)} %get-tuple-element.31), channel_id=1, source_target_pairs={{16,0},{20,4},{24,8},{28,12},{17,1},{21,5},{25,9},{29,13},{18,2},{... | collective-permute-start | bytes 1179656 | tf_op jit(solution)/shard_map/ppermute | solution.py:19
  344.9 14.5 %collective-permute-start.11 = (bf16[4,6,16,512]{3,2,1,0:T(8,128)(2,1)S(1)}, bf16[4,6,16,512]{3,2,1,0:T(8,128)(2,1)S(1)}, u32[]{:S(2)}, u32[]{:S(2)}) collective-permute-start(bf16[4,6,16,512]{3,2,1,0:T(8,128)(2,1)S(1)} %get-tuple-element.31), channel_id=1, source_target_pairs={{20,0},{24,4},{28,8},{21,1},{25,5},{29,9},{22,2},{26,6},{30,10},{2... | collective-permute-start | bytes 1179656 | tf_op jit(solution)/shard_map/ppermute | solution.py:19
  346.2 21.6 %collective-permute-start.9 = (bf16[4,6,16,512]{3,2,1,0:T(8,128)(2,1)S(1)}, bf16[4,6,16,512]{3,2,1,0:T(8,128)(2,1)S(1)}, u32[]{:S(2)}, u32[]{:S(2)}) collective-permute-start(bf16[4,6,16,512]{3,2,1,0:T(8,128)(2,1)S(1)} %get-tuple-element.31), channel_id=1, source_target_pairs={{12,0},{16,4},{20,8},{24,12},{28,16},{13,1},{17,5},{21,9},{25,13},... | collective-permute-start | bytes 1179656 | tf_op jit(solution)/shard_map/ppermute | solution.py:19
  348.8 20.5 %collective-permute-start.6 = (bf16[4,6,16,512]{3,2,1,0:T(8,128)(2,1)}, bf16[4,6,16,512]{3,2,1,0:T(8,128)(2,1)}, u32[]{:S(2)}, u32[]{:S(2)}) collective-permute-start(bf16[4,6,16,512]{3,2,1,0:T(8,128)(2,1)} %get-tuple-element.30), channel_id=1, source_target_pairs={{0,12},{4,16},{8,20},{12,24},{16,28},{1,13},{5,17},{9,21},{13,25},... | collective-permute-start | bytes 1179656 | tf_op jit(solution)/shard_map/ppermute | solution.py:19
  350.1 42.6 %collective-permute-start.7 = (bf16[4,6,16,512]{3,2,1,0:T(8,128)(2,1)}, bf16[4,6,16,512]{3,2,1,0:T(8,128)(2,1)}, u32[]{:S(2)}, u32[]{:S(2)}) collective-permute-start(bf16[4,6,16,512]{3,2,1,0:T(8,128)(2,1)} %get-tuple-element.30), channel_id=1, source_target_pairs={{0,16},{4,20},{8,24},{12,28},{1,17},{5,21},{9,25},{13,29},{2,18},{... | collective-permute-start | bytes 1179656 | tf_op jit(solution)/shard_map/ppermute | solution.py:19
  351.4 41.2 %collective-permute-start.8 = (bf16[4,6,16,512]{3,2,1,0:T(8,128)(2,1)}, bf16[4,6,16,512]{3,2,1,0:T(8,128)(2,1)}, u32[]{:S(2)}, u32[]{:S(2)}) collective-permute-start(bf16[4,6,16,512]{3,2,1,0:T(8,128)(2,1)} %get-tuple-element.30), channel_id=1, source_target_pairs={{0,20},{4,24},{8,28},{1,21},{5,25},{9,29},{2,22},{6,26},{10,30},{3... | collective-permute-start | bytes 1179656 | tf_op jit(solution)/shard_map/ppermute | solution.py:19
  369.3 26.0 %copy-start.6 = (pred[4]{0:T(512)(128)(4,1)S(1)}, pred[4]{0:T(512)(128)(4,1)}, u32[]{:S(2)}) copy-start(pred[4]{0:T(512)(128)(4,1)} %get-tuple-element.42) | copy-start | bytes 16
  395.3 1.7 copy-start.8
  (1 other events, 0.7 us)
Sparse Core Ops, SparseCore 0:
  8.9 35.8 all-gather.3
  46.8 96.8 all-gather.5
  145.9 47.5 all-gather.7
  200.9 72.7 reduce-scatter.1
where the time goes:
time: 406 us; the launch traced here: 405 us
  waiting for transfers between devices  292 us (72%)
  starting transfers between devices  29.2 us (7%)
  other arithmetic  28 us (7%)
  local copies, waits for them, and re-layouts  21.6 us (5%)
  matrix products  19.6 us (5%)
  between operations  14.2 us (3%)
    all_gather x1, waiting for transfers between devices, attend(): weight_piece = lax.all_gather(qkv_weight, 'region', axis=0, tiled=True)  91.2 us
    reduce_scatter x1, waiting for transfers between devices, attend(): lax.psum_scatter(partial_out, 'mp', scatter_dimension=1, tiled=True)  70.6 us
    ppermute x12, waiting for transfers between devices, from_behind(): return lax.ppermute(block, axis, route)  70.6 us
    all_gather x1, waiting for transfers between devices, attend(): gathered = lax.all_gather(local_rows, 'mp', axis=2, tiled=True)  34.3 us
    ppermute x12, starting transfers between devices, from_behind(): return lax.ppermute(block, axis, route)  29.1 us
    all_gather x1, waiting for transfers between devices, attend(): lax.all_gather(out_weight, 'region', axis=0, tiled=True)  24 us
    dot_general x1, matrix products, attend(): jnp.dot(hidden, flat_piece, preferred_element_type=jnp.float32)  11.3 us
  transfers between devices with their start and end apart: 16, of which 10 were waited for; matrix products, arithmetic and copies ran while one was open for 11% of the time, Pallas kernels for 0%

commit v1 on v0

v1 whole, which is shorter than its diff:
```python
import functools
import math

import jax
import jax.numpy as jnp
from jax import lax
from jax.experimental import pallas as pl
from jax.experimental.pallas import tpu as pltpu
from jax.sharding import PartitionSpec as P

HDIM = 128
S = 16
W = 6
TCOLS = 8
MESH = pl.DeviceIdType.MESH
F32 = jnp.float32
BF16 = jnp.bfloat16


def kernel(
    regions,
    counts_ref,
    blend_ref,
    tiles_ref,
    mod_ref,
    wqkv_ref,
    wout_ref,
    out_ref,
    slots,
    feats,
    mods,
    wq,
    wo,
    hidden,
    attended,
    part_near,
    part_far,
    from_core,
    from_far,
    updated,
    side,
    strips,
    finished,
    partner_done,
    swap_send,
    swap_recv,
    gather_send,
    gather_recv,
    line_send,
    line_recv,
    sum_send,
    sum_recv,
    edge_send,
    edge_recv,
):
    planes = regions // 2
    region = lax.axis_index("region")
    mp = lax.axis_index("mp")
    plane = region // 2
    x = region % 2
    xo = 1 - x
    partner = plane * 2 + xo
    core = mp % 2
    yy = mp // 2
    mp_core = yy * 2 + (1 - core)
    mp_y = (1 - yy) * 2 + core
    nslot, tok, wide = tiles_ref.shape
    fb = wide // 2
    rows = wqkv_ref.shape[1]
    down = TCOLS // nslot
    mine = mp * 2 + x
    has_up = plane > 0
    has_down = plane < planes - 1
    far_up = plane >= down
    far_down = plane < planes - down

    barrier = pltpu.get_barrier_semaphore()

    def greet(r, m):
        pl.semaphore_signal(barrier, inc=1, device_id=(r, m), device_id_type=MESH)

    greet(region, mp_core)
    greet(region, mp_y)
    greet(partner, mp)
    greet(partner, mp_y)
    for cond, step in ((has_up, -2), (has_down, 2), (far_up, -2 * down), (far_down, 2 * down)):

        @pl.when(cond)
        def _(step=step):
            greet(region + step, mp)

    arrivals = (
        4
        + has_up.astype(jnp.int32)
        + has_down.astype(jnp.int32)
        + far_up.astype(jnp.int32)
        + far_down.astype(jnp.int32)
    )
    pl.semaphore_wait(barrier, arrivals)

    def remote(src, dst, ssem, rsem, r, m):
        return pltpu.make_async_remote_copy(
            src_ref=src, dst_ref=dst, send_sem=ssem, recv_sem=rsem, device_id=(r, m), device_id_type=MESH
        )

    def block(buf, r):
        return buf.at[pl.ds(pl.multiple_of(r * rows, rows), rows)]

    def swap(i, src, dst):
        return remote(src, dst, swap_send.at[i], swap_recv.at[i], partner, mp)

    half_o = pl.ds(pl.multiple_of(xo * fb, fb), fb)
    half_m = pl.ds(pl.multiple_of(x * fb, fb), fb)

    def swaps(r, g):
        return (
            swap(0, wqkv_ref.at[xo], block(wq, r)),
            swap(1, tiles_ref.at[:, :, half_o], slots.at[g]),
            swap(2, mod_ref, mods.at[g]),
            swap(3, wout_ref.at[xo], block(wo, r)),
        )

    out_swaps = swaps(region, x)
    in_swaps = swaps(partner, xo)
    for c in out_swaps:
        c.start()
    block(wq, region)[...] = wqkv_ref[x]
    block(wo, region)[...] = wout_ref[x]
    mods[x] = mod_ref[...]
    slots[x] = tiles_ref[:, :, half_m]

    def line(buf, kind, way, s, h, q):
        ref = block(buf, 2 * q + h)
        step = 2 if way == 0 else -2
        return remote(
            ref, ref, line_send.at[way, kind, s, h], line_recv.at[way, kind, s, h], region + step, mp
        )

    def line_do(buf, kind, s, h, act):
        @pl.when(has_down & (plane - s >= 0))
        def _():
            act(line(buf, kind, 0, s, h, plane - s))

        @pl.when(has_up & (plane + s <= planes - 1))
        def _():
            act(line(buf, kind, 1, s, h, plane + s))

    def line_send_start(buf, kind, s, h):
        line_do(buf, kind, s, h, lambda c: c.start())

    def line_wait_recv(buf, kind, s):
        @pl.when(plane - s - 1 >= 0)
        def _():
            for h in range(2):
                line(buf, kind, 0, s, h, plane - s - 1).wait_recv()

        @pl.when(plane + s + 1 <= planes - 1)
        def _():
            for h in range(2):
                line(buf, kind, 1, s, h, plane + s + 1).wait_recv()

    def line_forward(buf, kind, s):
        line_wait_recv(buf, kind, s)

        @pl.when(s + 1 < planes - 1)
        def _():
            for h in range(2):
                line_send_start(buf, kind, s + 1, h)

    line_send_start(wq, 0, 0, x)
    in_swaps[0].wait_recv()
    line_send_start(wq, 0, 0, xo)

    in_swaps[1].wait_recv()
    even = counts_ref[2 * plane]
    own_count = counts_ref[region]
    for k in range(nslot):
        first = slots[0, k]
        second = slots[1, jnp.clip(k - even, 0, nslot - 1)]
        feats[mine, k] = jnp.where(k < even, first, second)

    def gather(i, b, r, m):
        return remote(feats.at[b], feats.at[b], gather_send.at[i], gather_recv.at[i], r, m)

    blocks = (mp * 2 + xo, mp_y * 2 + x, mp_y * 2 + xo)
    core_blocks = (mp_core * 2 + x, mp_core * 2 + xo, (3 - mp) * 2 + x, (3 - mp) * 2 + xo)
    sends = [
        gather(0, mine, partner, mp),
        gather(1, mine, region, mp_y),
        gather(2, mine, partner, mp_y),
        gather(3, mine, region, mp_core),
    ]
    for c in (sends[2], sends[0], sends[1], sends[3]):
        c.start()
    line_forward(wq, 0, 0)
    for i in range(3):
        gather(i, blocks[i], region, mp_core).wait_recv()
        c = gather(4 + i, blocks[i], region, mp_core)
        c.start()
        sends.append(c)
    in_swaps[2].wait_recv()
    in_swaps[3].wait_recv()
    for i in range(4):
        gather(3 + i, core_blocks[i], region, mp_core).wait_recv()

    nblock = feats.shape[0]
    inv = 1.0 / (nblock * fb)
    mod_e = mods[0].astype(F32)
    mod_d = mods[1].astype(F32)

    def normalise(t, _):
        total = jnp.zeros((tok, 1), F32)
        for b in range(nblock):
            total = total + jnp.sum(feats[b, t].astype(F32), axis=1, keepdims=True)
        mean = total * inv
        total = jnp.zeros((tok, 1), F32)
        for b in range(nblock):
            c = feats[b, t].astype(F32) - mean
            total = total + jnp.sum(c * c, axis=1, keepdims=True)
        scale = lax.rsqrt(total * inv + 1e-06)
        mod = jnp.where(t < even, mod_e, mod_d)
        for b in range(nblock):
            at = slice(b * fb, (b + 1) * fb)
            c = (feats[b, t].astype(F32) - mean) * scale
            hidden[t, :, at] = (c * (1.0 + mod[1:2, at]) + mod[0:1, at]).astype(BF16)
        return 0

    @pl.when(planes > 2)
    def _():
        line_forward(wq, 0, 1)

    lax.fori_loop(0, nslot, normalise, 0)

    def more(s, _):
        line_forward(wq, 0, s)
        return 0

    lax.fori_loop(2, planes - 1, more, 0)
    for h in range(2):
        line_send_start(wo, 1, 0, h)

    heads = fb // HDIM

    def attend(t, _):
        proj = jnp.dot(hidden[t], wq[...], preferred_element_type=F32).astype(BF16)
        for h in range(heads):
            q = proj[:, h * HDIM : (h + 1) * HDIM]
            k = proj[:, fb + h * HDIM : fb + (h + 1) * HDIM]
            v = proj[:, 2 * fb + h * HDIM : 2 * fb + (h + 1) * HDIM]
            scores = lax.dot_general(q, k, (((1,), (1,)), ((), ())), preferred_element_type=F32)
            scores = scores * (1.0 / math.sqrt(HDIM))
            e = jnp.exp(scores - jnp.max(scores, axis=-1, keepdims=True))
            p = (e / jnp.sum(e, axis=-1, keepdims=True)).astype(BF16)
            attended[t, :, h * HDIM : (h + 1) * HDIM] = jnp.dot(
                p, v, preferred_element_type=F32
            ).astype(BF16)

        @pl.when(t < planes - 1)
        def _():
            line_forward(wo, 1, t)

        return 0

    lax.fori_loop(0, nslot, attend, 0)

    def rest(s, _):
        line_forward(wo, 1, s)
        return 0

    if planes - 1 > nslot:
        lax.fori_loop(nslot, planes - 1, rest, 0)

    def product(b, t):
        w = wo[pl.ds(pl.multiple_of(b * fb, fb), fb)]
        return lax.dot_general(attended[t], w, (((1,), (1,)), ((), ())), preferred_element_type=F32)

    dests = ((xo, mp_y), (x, mp_y), (xo, mp), (x, mp))

    def core_sum(i):
        return remote(
            part_near.at[i], from_core.at[i], sum_send.at[i], sum_recv.at[i], region, mp_core
        )

    def far_sum(i):
        dx, dm = dests[i]
        return remote(
            part_far.at[i], from_far.at[i], sum_send.at[4 + i], sum_recv.at[4 + i], plane * 2 + dx, dm
        )

    for i, (dx, dm) in enumerate(dests):
        b = (dm + 1 - 2 * core) * 2 + dx

        def near(t, _, i=i, b=b):
            part_near[i, t] = product(b, t).astype(BF16)
            return 0

        lax.fori_loop(0, nslot, near, 0)
        core_sum(i).start()
    for i, (dx, dm) in enumerate(dests[:3]):
        b = dm * 2 + dx
        core_sum(i).wait_recv()

        def far(t, _, i=i, b=b):
            part_far[i, t] = (product(b, t) + from_core[i, t].astype(F32)).astype(BF16)
            return 0

        lax.fori_loop(0, nslot, far, 0)
        far_sum(i).start()
    core_sum(3).wait_recv()
    for i in range(3):
        far_sum(i).wait_recv()
    at_m = pl.ds(pl.multiple_of(mine * fb, fb), fb)
    gate_e = mods[0, :, at_m].astype(F32)[2:3]
    gate_d = mods[1, :, at_m].astype(F32)[2:3]

    def update(t, _):
        total = product(mine, t) + from_core[3, t].astype(F32)
        for i in range(3):
            total = total + from_far[i, t].astype(F32)
        gate = jnp.where(t < even, gate_e, gate_d)
        updated[t] = (feats[mine, t].astype(F32) + gate * total).astype(BF16)
        return 0

    lax.fori_loop(0, nslot, update, 0)

    odd = plane % 2
    edge_tile = (1 - odd) * (nslot - 1)
    to_side = remote(
        updated.at[edge_tile],
        side,
        edge_send.at[0],
        edge_recv.at[0],
        region + 2 - 4 * odd,
        mp,
    )
    to_side.start()
    token = lax.broadcasted_iota(jnp.int32, (tok, fb), 0)
    col = token % S
    share = jnp.zeros((tok, fb), F32)
    for k in range(W):
        share = jnp.where((col == k) | (col == S - W + k), blend_ref[k], share)
    near_cols = col < W
    far_cols = col >= S - W
    to_side.wait_recv()
    plain = [updated[k].astype(F32) for k in range(nslot)]
    edge = side[...].astype(F32)
    for k in range(nslot):
        own = plain[k]
        if k > 0:
            left, has_left = plain[k - 1], True
        else:
            left, has_left = edge, odd == 1
        if k < nslot - 1:
            right, has_right = plain[k + 1], True
        else:
            right, has_right = edge, odd == 0
        left = pltpu.roll(left, tok - (S - W), 0)
        right = pltpu.roll(right, S - W, 0)
        new = jnp.where(near_cols & has_left, (1.0 - share) * left + share * own, own)
        new = jnp.where(far_cols & has_right, (1.0 - share) * own + share * right, new)
        finished[k] = new.astype(BF16)

    reach = W * S
    low = pl.ds(0, reach)
    high = pl.ds(tok - reach, reach)

    def to_above():
        return remote(
            finished.at[:, low],
            strips.at[0],
            edge_send.at[1],
            edge_recv.at[1],
            region - 2 * down,
            mp,
        )

    def to_below():
        return remote(
            finished.at[:, high],
            strips.at[1],
            edge_send.at[2],
            edge_recv.at[2],
            region + 2 * down,
            mp,
        )

    @pl.when(far_up)
    def _():
        to_above().start()

    @pl.when(far_down)
    def _():
        to_below().start()

    row = lax.broadcasted_iota(jnp.int32, (reach, fb), 0) // S
    vshare = jnp.zeros((reach, fb), F32)
    for k in range(W):
        vshare = jnp.where(row == k, blend_ref[k], vshare)

    @pl.when(far_up)
    def _():
        to_above().wait_send()
        to_below().wait_recv()
        for k in range(nslot):
            own = finished[k, low].astype(F32)
            finished[k, low] = ((1.0 - vshare) * strips[1, k].astype(F32) + vshare * own).astype(BF16)

    @pl.when(far_down)
    def _():
        to_below().wait_send()
        to_above().wait_recv()
        for k in range(nslot):
            own = finished[k, high].astype(F32)
            finished[k, high] = ((1.0 - vshare) * own + vshare * strips[0, k].astype(F32)).astype(BF16)

    last = remote(finished, partner_done, edge_send.at[3], edge_recv.at[3], partner, mp)
    last.start()
    start = x * even
    for s in range(nslot):
        got = finished[jnp.clip(start + s, 0, nslot - 1)]
        out_ref[s, :, half_m] = jnp.where(s < own_count, got, jnp.zeros_like(got))
    last.wait_recv()
    for s in range(nslot):
        got = partner_done[jnp.clip(start + s, 0, nslot - 1)]
        out_ref[s, :, half_o] = jnp.where(s < own_count, got, jnp.zeros_like(got))

    last.wait_send()
    to_side.wait_send()
    for c in out_swaps:
        c.wait_send()
    for c in sends:
        c.wait_send()
    for i in range(4):
        core_sum(i).wait_send()
    for i in range(3):
        far_sum(i).wait_send()

    def drain(s, _):
        for kind, buf in ((0, wq), (1, wo)):
            for h in range(2):
                line_do(buf, kind, s, h, lambda c: c.wait_send())
        return 0

    lax.fori_loop(0, planes - 1, drain, 0)


def on_device(regions, tile_data, tile_counts, modulation, qkv_weight, out_weight, blend_weights):
    nslot, tok, wide = tile_data.shape
    rows, kinds, _ = qkv_weight.shape
    fb = wide // 2
    width = modulation.shape[2]
    nblock = width // fb
    planes = regions // 2
    wqkv = qkv_weight.reshape(rows, kinds, 2, fb).transpose(2, 0, 1, 3).reshape(2, rows, kinds * fb)
    wout = out_weight.reshape(rows, 2, fb).transpose(1, 0, 2)
    mod = jnp.pad(modulation[0], ((0, 13), (0, 0)))
    vmem = pl.BlockSpec(memory_space=pltpu.VMEM)
    smem = pl.BlockSpec(memory_space=pltpu.SMEM)
    dma = pltpu.SemaphoreType.DMA
    return pl.pallas_call(
        functools.partial(kernel, regions),
        out_shape=jax.ShapeDtypeStruct(tile_data.shape, BF16),
        in_specs=[smem, smem, vmem, vmem, vmem, vmem],
        out_specs=vmem,
        scratch_shapes=[
            pltpu.VMEM((2, nslot, tok, fb), BF16),
            pltpu.VMEM((nblock, nslot, tok, fb), BF16),
            pltpu.VMEM((2, 16, width), BF16),
            pltpu.VMEM((width, kinds * fb), BF16),
            pltpu.VMEM((width, fb), BF16),
            pltpu.VMEM((nslot, tok, width), BF16),
            pltpu.VMEM((nslot, tok, fb), BF16),
            pltpu.VMEM((4, nslot, tok, fb), BF16),
            pltpu.VMEM((3, nslot, tok, fb), BF16),
            pltpu.VMEM((4, nslot, tok, fb), BF16),
            pltpu.VMEM((3, nslot, tok, fb), BF16),
            pltpu.VMEM((nslot, tok, fb), BF16),
            pltpu.VMEM((tok, fb), BF16),
            pltpu.VMEM((2, nslot, W * S, fb), BF16),
            pltpu.VMEM((nslot, tok, fb), BF16),
            pltpu.VMEM((nslot, tok, fb), BF16),
            dma((4,)),
            dma((4,)),
            dma((7,)),
            dma((7,)),
            dma((2, 2, planes - 1, 2)),
            dma((2, 2, planes - 1, 2)),
            dma((7,)),
            dma((7,)),
            dma((4,)),
            dma((4,)),
        ],
        compiler_params=pltpu.CompilerParams(
            collective_id=0, has_side_effects=True, vmem_limit_bytes=56 * 1024 * 1024
        ),
    )(tile_counts, blend_weights, tile_data, mod, wqkv, wout)


def solution(mesh):
    return jax.shard_map(
        functools.partial(on_device, mesh.shape["region"]),
        mesh=mesh,
        in_specs=(
            P("region", None, "mp"),
            P(),
            P("region", None, None),
            P("region", None, "mp"),
            P("region", "mp"),
            P(),
        ),
        out_specs=P("region", None, "mp"),
        check_vma=False,
    )
```

time: 406 us -> 166 us (0.41)
  the two profiles are of different devices: /device:TPU:27 before, /device:TPU:0 now
where the time goes in v1:
time: 166 us
  Pallas kernels  159 us (96%)
  local copies, waits for them, and re-layouts  7.09 us (4%)
    pallas_call x1, Pallas kernels, on_device(): pl.pallas_call(functools.partial(kernel, regions), out_shape=jax.ShapeDty...  159 us
    unnamed x5, local copies, waits for them, and re-layouts  3.62 us

profile of v1, /device:TPU:0, one launch (start us, length us, event | category | flops | bytes accessed | tf_op | source)
XLA Modules:
  0.0 166.0 jit_solution(561150147874563149)
XLA Ops:
  0.0 0.0 copy-start
  0.0 1.4 pad.4.mod_ref
  1.4 1.1 copy.13
  2.5 0.8 copy.14
  3.4 0.0 copy-done
  3.4 0.3 copy.11
  3.6 0.1 copy.12
  3.7 1.2 copy.15.wqkv_ref
  4.8 158.8 %shard_map.64 = bf16[4,256,512]{2,1,0:T(8,128)(2,1)} custom-call(s32[8]{0:T(128)} %counts_ref.1, f32[6]{0:T(128)} %blend_ref.1, bf16[4,256,512]{2,1,0:T(8,128)(2,1)} %tiles_ref.1, bf16[16,2048]{1,0:T(8,128)(2,1)} %pad.4.mod_ref, bf16[2,256,768]{2,1,0:T(8,128)(2,1)} %copy.15.wqkv_ref, bf16[2,256,256]{2,1,0:T(8,128)(2,1)} %bitcast.9), custom_call_target="tpu_custom_call" | custom-call | tf_op jit(solution)/shard_map/pallas_call | solution.py:460
  163.7 2.3 %copy.17 = bf16[4,256,512]{2,1,0:T(8,128)(2,1)} copy(bf16[4,256,512]{2,1,0:T(8,128)(2,1)} %shard_map.64) | data formatting | bytes 2097152
Async XLA Ops:
  0.0 3.4 %copy-start = (bf16[256,3,512]{2,0,1:T(8,128)(2,1)S(1)}, bf16[256,3,512]{2,0,1:T(8,128)(2,1)}, u32[]{:S(2)}) copy-start(bf16[256,3,512]{2,0,1:T(8,128)(2,1)} %param.9) | copy-start | bytes 2359300

commit v2 on v1

--- a/solution.py
+++ b/solution.py
@@ -29,6 +29,7 @@
     slots,
     feats,
     mods,
+    stage,
     wq,
     wo,
     hidden,
@@ -48,10 +49,16 @@
     gather_recv,
     line_send,
     line_recv,
+    near_send,
+    near_recv,
     sum_send,
     sum_recv,
     edge_send,
     edge_recv,
+    strip_send,
+    strip_recv,
+    last_send,
+    last_recv,
 ):
     planes = regions // 2
     region = lax.axis_index("region")
@@ -66,7 +73,8 @@
     mp_y = (1 - yy) * 2 + core
     nslot, tok, wide = tiles_ref.shape
     fb = wide // 2
-    rows = wqkv_ref.shape[1]
+    rows = wqkv_ref.shape[0]
+    kinds = wqkv_ref.shape[1] // wide
     down = TCOLS // nslot
     mine = mp * 2 + x
     has_up = plane > 0
@@ -114,20 +122,21 @@
 
     def swaps(r, g):
         return (
-            swap(0, wqkv_ref.at[xo], block(wq, r)),
+            swap(0, stage, block(wq, r)),
             swap(1, tiles_ref.at[:, :, half_o], slots.at[g]),
-            swap(2, mod_ref, mods.at[g]),
-            swap(3, wout_ref.at[xo], block(wo, r)),
+            swap(2, mods.at[g], mods.at[g]),
+            swap(3, wout_ref.at[:, half_o], block(wo, r)),
         )
 
     out_swaps = swaps(region, x)
     in_swaps = swaps(partner, xo)
-    for c in out_swaps:
-        c.start()
-    block(wq, region)[...] = wqkv_ref[x]
-    block(wo, region)[...] = wout_ref[x]
-    mods[x] = mod_ref[...]
-    slots[x] = tiles_ref[:, :, half_m]
+    for k in range(kinds):
+        at = pl.ds(pl.multiple_of(k * wide + xo * fb, fb), fb)
+        stage[:, k * fb : (k + 1) * fb] = wqkv_ref[:, at]
+    out_swaps[0].start()
+    for k in range(kinds):
+        at = pl.ds(pl.multiple_of(k * wide + x * fb, fb), fb)
+        wq[pl.ds(pl.multiple_of(region * rows, rows), rows), k * fb : (k + 1) * fb] = wqkv_ref[:, at]
 
     def line(buf, kind, way, s, h, q):
         ref = block(buf, 2 * q + h)
@@ -168,8 +177,13 @@
                 line_send_start(buf, kind, s + 1, h)
 
     line_send_start(wq, 0, 0, x)
+    block(wo, region)[...] = wout_ref[:, half_m]
+    mods[x, 0:3, :] = mod_ref[0]
+    slots[x] = tiles_ref[:, :, half_m]
     in_swaps[0].wait_recv()
     line_send_start(wq, 0, 0, xo)
+    for c in out_swaps[1:]:
+        c.start()
 
     in_swaps[1].wait_recv()
     even = counts_ref[2 * plane]
@@ -193,13 +207,19 @@
     for c in (sends[2], sends[0], sends[1], sends[3]):
         c.start()
     line_forward(wq, 0, 0)
+    in_swaps[2].wait_recv()
+    in_swaps[3].wait_recv()
+    for h in range(2):
+        line_send_start(wo, 1, 0, h)
+
+    line_forward(wq, 0, 1)
+    if planes > 3:
+        line_forward(wo, 1, 0)
     for i in range(3):
         gather(i, blocks[i], region, mp_core).wait_recv()
         c = gather(4 + i, blocks[i], region, mp_core)
         c.start()
         sends.append(c)
-    in_swaps[2].wait_recv()
-    in_swaps[3].wait_recv()
     for i in range(4):
         gather(3 + i, core_blocks[i], region, mp_core).wait_recv()
 
@@ -225,19 +245,15 @@
             hidden[t, :, at] = (c * (1.0 + mod[1:2, at]) + mod[0:1, at]).astype(BF16)
         return 0
 
-    @pl.when(planes > 2)
-    def _():
-        line_forward(wq, 0, 1)
-
     lax.fori_loop(0, nslot, normalise, 0)
 
     def more(s, _):
+        line_forward(wo, 1, s - 1)
         line_forward(wq, 0, s)
         return 0
 
-    lax.fori_loop(2, planes - 1, more, 0)
-    for h in range(2):
-        line_send_start(wo, 1, 0, h)
+    lax.fori_loop(2, planes - 2, more, 0)
+    line_forward(wq, 0, planes - 2)
 
     heads = fb // HDIM
 
@@ -255,20 +271,21 @@
                 p, v, preferred_element_type=F32
             ).astype(BF16)
 
-        @pl.when(t < planes - 1)
-        def _():
-            line_forward(wo, 1, t)
-
         return 0
 
-    lax.fori_loop(0, nslot, attend, 0)
-
-    def rest(s, _):
-        line_forward(wo, 1, s)
+    odd = plane % 2
+
+    def tile_at(i):
+        return i * odd + (nslot - 1 - i) * (1 - odd)
+
+    def attend_at(i, _):
+        attend(tile_at(i), 0)
         return 0
 
-    if planes - 1 > nslot:
-        lax.fori_loop(nslot, planes - 1, rest, 0)
+    attend_at(0, 0)
+    line_forward(wo, 1, planes - 3)
+    lax.fori_loop(1, nslot - 1, attend_at, 0)
+    line_forward(wo, 1, planes - 2)
 
     def product(b, t):
         w = wo[pl.ds(pl.multiple_of(b * fb, fb), fb)]
@@ -277,163 +294,191 @@
     dests = ((xo, mp_y), (x, mp_y), (xo, mp), (x, mp))
 
     def core_sum(i):
+        t = tile_at(i)
         return remote(
-            part_near.at[i], from_core.at[i], sum_send.at[i], sum_recv.at[i], region, mp_core
-        )
-
-    def far_sum(i):
-        dx, dm = dests[i]
+            part_near.at[t], from_core.at[t], near_send.at[i], near_recv.at[i], region, mp_core
+        )
+
+    def far_sum(i, d):
+        dx, dm = dests[d]
+        t = tile_at(i)
         return remote(
-            part_far.at[i], from_far.at[i], sum_send.at[4 + i], sum_recv.at[4 + i], plane * 2 + dx, dm
-        )
-
-    for i, (dx, dm) in enumerate(dests):
-        b = (dm + 1 - 2 * core) * 2 + dx
-
-        def near(t, _, i=i, b=b):
-            part_near[i, t] = product(b, t).astype(BF16)
-            return 0
-
-        lax.fori_loop(0, nslot, near, 0)
+            part_far.at[d, t],
+            from_far.at[d, t],
+            sum_send.at[d, i],
+            sum_recv.at[d, i],
+            plane * 2 + dx,
+            dm,
+        )
+
+    def near(i):
+        t = tile_at(i)
+        for d, (dx, dm) in enumerate(dests):
+            part_near[t, d] = product((dm + 1 - 2 * core) * 2 + dx, t).astype(BF16)
         core_sum(i).start()
-    for i, (dx, dm) in enumerate(dests[:3]):
-        b = dm * 2 + dx
+
+    def far(i):
+        t = tile_at(i)
         core_sum(i).wait_recv()
-
-        def far(t, _, i=i, b=b):
-            part_far[i, t] = (product(b, t) + from_core[i, t].astype(F32)).astype(BF16)
-            return 0
-
-        lax.fori_loop(0, nslot, far, 0)
-        far_sum(i).start()
-    core_sum(3).wait_recv()
-    for i in range(3):
-        far_sum(i).wait_recv()
+        for d, (dx, dm) in enumerate(dests[:3]):
+            part_far[d, t] = (product(dm * 2 + dx, t) + from_core[t, d].astype(F32)).astype(BF16)
+            far_sum(i, d).start()
+
+    near(0)
+    attend(tile_at(nslot - 1), 0)
+    for i in range(1, nslot):
+        near(i)
+        far(i - 1)
+    far(nslot - 1)
+
     at_m = pl.ds(pl.multiple_of(mine * fb, fb), fb)
     gate_e = mods[0, :, at_m].astype(F32)[2:3]
     gate_d = mods[1, :, at_m].astype(F32)[2:3]
 
-    def update(t, _):
-        total = product(mine, t) + from_core[3, t].astype(F32)
-        for i in range(3):
-            total = total + from_far[i, t].astype(F32)
+    def update(i):
+        t = tile_at(i)
+        total = product(mine, t) + from_core[t, 3].astype(F32)
+        for d in range(3):
+            far_sum(i, d).wait_recv()
+            total = total + from_far[d, t].astype(F32)
         gate = jnp.where(t < even, gate_e, gate_d)
         updated[t] = (feats[mine, t].astype(F32) + gate * total).astype(BF16)
-        return 0
-
-    lax.fori_loop(0, nslot, update, 0)
-
-    odd = plane % 2
-    edge_tile = (1 - odd) * (nslot - 1)
+
     to_side = remote(
-        updated.at[edge_tile],
+        updated.at[tile_at(0)],
         side,
         edge_send.at[0],
         edge_recv.at[0],
         region + 2 - 4 * odd,
         mp,
     )
-    to_side.start()
-    token = lax.broadcasted_iota(jnp.int32, (tok, fb), 0)
-    col = token % S
+    col = lax.broadcasted_iota(jnp.int32, (tok, fb), 0) % S
     share = jnp.zeros((tok, fb), F32)
     for k in range(W):
         share = jnp.where((col == k) | (col == S - W + k), blend_ref[k], share)
     near_cols = col < W
     far_cols = col >= S - W
-    to_side.wait_recv()
-    plain = [updated[k].astype(F32) for k in range(nslot)]
-    edge = side[...].astype(F32)
-    for k in range(nslot):
-        own = plain[k]
-        if k > 0:
-            left, has_left = plain[k - 1], True
+
+    def across(i):
+        t = tile_at(i)
+        own = updated[t].astype(F32)
+        if i > 0:
+            before = updated[tile_at(i - 1)].astype(F32)
         else:
-            left, has_left = edge, odd == 1
-        if k < nslot - 1:
-            right, has_right = plain[k + 1], True
+            before = side[...].astype(F32)
+        if i < nslot - 1:
+            after = updated[tile_at(i + 1)].astype(F32)
+            has_left = has_right = True
         else:
-            right, has_right = edge, odd == 0
+            after = own
+            has_left, has_right = odd == 1, odd == 0
+        left = jnp.where(odd == 1, before, after)
+        right = jnp.where(odd == 1, after, before)
         left = pltpu.roll(left, tok - (S - W), 0)
         right = pltpu.roll(right, S - W, 0)
         new = jnp.where(near_cols & has_left, (1.0 - share) * left + share * own, own)
         new = jnp.where(far_cols & has_right, (1.0 - share) * own + share * right, new)
-        finished[k] = new.astype(BF16)
+        finished[t] = new.astype(BF16)
+
+        @pl.when(far_up)
+        def _():
+            to_above(i).start()
+
+        @pl.when(far_down)
+        def _():
+            to_below(i).start()
 
     reach = W * S
     low = pl.ds(0, reach)
     high = pl.ds(tok - reach, reach)
 
-    def to_above():
+    def to_above(i):
+        t = tile_at(i)
         return remote(
-            finished.at[:, low],
-            strips.at[0],
-            edge_send.at[1],
-            edge_recv.at[1],
+            finished.at[t, low],
+            strips.at[0, t],
+            strip_send.at[0, i],
+            strip_recv.at[0, i],
             region - 2 * down,
             mp,
         )
 
-    def to_below():
+    def to_below(i):
+        t = tile_at(i)
         return remote(
-            finished.at[:, high],
-            strips.at[1],
-            edge_send.at[2],
-            edge_recv.at[2],
+            finished.at[t, high],
+            strips.at[1, t],
+            strip_send.at[1, i],
+            strip_recv.at[1, i],
             region + 2 * down,
             mp,
         )
-
-    @pl.when(far_up)
-    def _():
-        to_above().start()
-
-    @pl.when(far_down)
-    def _():
-        to_below().start()
 
     row = lax.broadcasted_iota(jnp.int32, (reach, fb), 0) // S
     vshare = jnp.zeros((reach, fb), F32)
     for k in range(W):
         vshare = jnp.where(row == k, blend_ref[k], vshare)
 
-    @pl.when(far_up)
-    def _():
-        to_above().wait_send()
-        to_below().wait_recv()
-        for k in range(nslot):
-            own = finished[k, low].astype(F32)
-            finished[k, low] = ((1.0 - vshare) * strips[1, k].astype(F32) + vshare * own).astype(BF16)
-
-    @pl.when(far_down)
-    def _():
-        to_below().wait_send()
-        to_above().wait_recv()
-        for k in range(nslot):
-            own = finished[k, high].astype(F32)
-            finished[k, high] = ((1.0 - vshare) * own + vshare * strips[0, k].astype(F32)).astype(BF16)
-
-    last = remote(finished, partner_done, edge_send.at[3], edge_recv.at[3], partner, mp)
-    last.start()
+    def to_owner(i):
+        t = tile_at(i)
+        return remote(
+            finished.at[t], partner_done.at[t], last_send.at[i], last_recv.at[i], partner, mp
+        )
+
+    def downward(i):
+        t = tile_at(i)
+
+        @pl.when(far_up)
+        def _():
+            to_above(i).wait_send()
+            to_below(i).wait_recv()
+            own = finished[t, low].astype(F32)
+            other = strips[1, t].astype(F32)
+            finished[t, low] = ((1.0 - vshare) * other + vshare * own).astype(BF16)
+
+        @pl.when(far_down)
+        def _():
+            to_below(i).wait_send()
+            to_above(i).wait_recv()
+            own = finished[t, high].astype(F32)
+            other = strips[0, t].astype(F32)
+            finished[t, high] = ((1.0 - vshare) * own + vshare * other).astype(BF16)
+
+        to_owner(i).start()
+
+    update(0)
+    to_side.start()
+    for i in range(1, nslot):
+        update(i)
+        if i == 1:
+            to_side.wait_recv()
+        across(i - 1)
+        if i > 1:
+            downward(i - 2)
+    across(nslot - 1)
+    downward(nslot - 2)
+    downward(nslot - 1)
+
     start = x * even
     for s in range(nslot):
         got = finished[jnp.clip(start + s, 0, nslot - 1)]
         out_ref[s, :, half_m] = jnp.where(s < own_count, got, jnp.zeros_like(got))
-    last.wait_recv()
+    for i in range(nslot):
+        to_owner(i).wait_recv()
     for s in range(nslot):
         got = partner_done[jnp.clip(start + s, 0, nslot - 1)]
         out_ref[s, :, half_o] = jnp.where(s < own_count, got, jnp.zeros_like(got))
 
-    last.wait_send()
     to_side.wait_send()
     for c in out_swaps:
         c.wait_send()
     for c in sends:
         c.wait_send()
-    for i in range(4):
+    for i in range(nslot):
+        to_owner(i).wait_send()
         core_sum(i).wait_send()
-    for i in range(3):
-        far_sum(i).wait_send()
+        for d in range(3):
+            far_sum(i, d).wait_send()
 
     def drain(s, _):
         for kind, buf in ((0, wq), (1, wo)):
@@ -451,9 +496,7 @@
     width = modulation.shape[2]
     nblock = width // fb
     planes = regions // 2
-    wqkv = qkv_weight.reshape(rows, kinds, 2, fb).transpose(2, 0, 1, 3).reshape(2, rows, kinds * fb)
-    wout = out_weight.reshape(rows, 2, fb).transpose(1, 0, 2)
-    mod = jnp.pad(modulation[0], ((0, 13), (0, 0)))
+    wqkv = qkv_weight.reshape(rows, kinds * wide)
     vmem = pl.BlockSpec(memory_space=pltpu.VMEM)
     smem = pl.BlockSpec(memory_space=pltpu.SMEM)
     dma = pltpu.SemaphoreType.DMA
@@ -466,13 +509,14 @@
             pltpu.VMEM((2, nslot, tok, fb), BF16),
             pltpu.VMEM((nblock, nslot, tok, fb), BF16),
             pltpu.VMEM((2, 16, width), BF16),
+            pltpu.VMEM((rows, kinds * fb), BF16),
             pltpu.VMEM((width, kinds * fb), BF16),
             pltpu.VMEM((width, fb), BF16),
             pltpu.VMEM((nslot, tok, width), BF16),
             pltpu.VMEM((nslot, tok, fb), BF16),
-            pltpu.VMEM((4, nslot, tok, fb), BF16),
+            pltpu.VMEM((nslot, 4, tok, fb), BF16),
             pltpu.VMEM((3, nslot, tok, fb), BF16),
-            pltpu.VMEM((4, nslot, tok, fb), BF16),
+            pltpu.VMEM((nslot, 4, tok, fb), BF16),
             pltpu.VMEM((3, nslot, tok, fb), BF16),
             pltpu.VMEM((nslot, tok, fb), BF16),
             pltpu.VMEM((tok, fb), BF16),
@@ -485,15 +529,21 @@
             dma((7,)),
             dma((2, 2, planes - 1, 2)),
             dma((2, 2, planes - 1, 2)),
-            dma((7,)),
-            dma((7,)),
-            dma((4,)),
-            dma((4,)),
+            dma((nslot,)),
+            dma((nslot,)),
+            dma((3, nslot)),
+            dma((3, nslot)),
+            dma((1,)),
+            dma((1,)),
+            dma((2, nslot)),
+            dma((2, nslot)),
+            dma((nslot,)),
+            dma((nslot,)),
         ],
         compiler_params=pltpu.CompilerParams(
             collective_id=0, has_side_effects=True, vmem_limit_bytes=56 * 1024 * 1024
         ),
-    )(tile_counts, blend_weights, tile_data, mod, wqkv, wout)
+    )(tile_counts, blend_weights, tile_data, modulation, wqkv, out_weight)
 
 
 def solution(mesh):

time: 166 us -> 126 us (0.76)
  Pallas kernels: 159 us -> 121 us
  local copies, waits for them, and re-layouts: 7.09 us -> 4.82 us
    pallas_call x1, Pallas kernels: 159 us -> 121 us  [on_device(): pl.pallas_call(functools.partial(kernel, regions), out_shape=jax.ShapeDty...]
    unnamed x5 -> x2, local copies, waits for them, and re-layouts: 3.62 us -> 3.66 us
where the time goes in v2:
time: 126 us; the launch traced here: 125 us
  Pallas kernels  121 us (96%)
  local copies, waits for them, and re-layouts  4.82 us (4%)
    pallas_call x1, Pallas kernels, on_device(): pl.pallas_call(functools.partial(kernel, regions), out_shape=jax.ShapeDty...  121 us
    unnamed x2, local copies, waits for them, and re-layouts  3.66 us

profile of v2, /device:TPU:0, one launch (start us, length us, event | category | flops | bytes accessed | tf_op | source)
XLA Modules:
  0.0 125.4 jit_solution(17737864828287285090)
XLA Ops:
  0.0 1.4 %copy.8 = bf16[256,3,512]{0,2,1:T(8,128)(2,1)S(1)} copy(bf16[256,3,512]{2,0,1:T(8,128)(2,1)} %param.9) | data formatting | bytes 1572864 | tf_op args[3]
  1.4 1.2 copy.9.wqkv_ref
  2.6 120.5 %shard_map.64 = bf16[4,256,512]{2,1,0:T(8,128)(2,1)} custom-call(s32[8]{0:T(128)} %counts_ref.1, f32[6]{0:T(128)} %blend_ref.1, bf16[4,256,512]{2,1,0:T(8,128)(2,1)} %tiles_ref.1, bf16[1,3,2048]{2,1,0:T(4,128)(2,1)} %mod_ref.1, bf16[256,1536]{1,0:T(8,128)(2,1)} %copy.9.wqkv_ref, bf16[256,512]{1,0:T(8,128)(2,1)} %wout_ref.1), custom_call_target="tpu_custom_call" | custom-call | tf_op jit(solution)/shard_map/pallas_call | solution.py:503
  123.1 2.3 %copy.11 = bf16[4,256,512]{2,1,0:T(8,128)(2,1)} copy(bf16[4,256,512]{2,1,0:T(8,128)(2,1)} %shard_map.64) | data formatting | bytes 2097152

commit v3 on v2

--- a/solution.py
+++ b/solution.py
@@ -49,6 +49,8 @@
     gather_recv,
     line_send,
     line_recv,
+    heads_send,
+    heads_recv,
     near_send,
     near_recv,
     sum_send,
@@ -125,7 +127,6 @@
             swap(0, stage, block(wq, r)),
             swap(1, tiles_ref.at[:, :, half_o], slots.at[g]),
             swap(2, mods.at[g], mods.at[g]),
-            swap(3, wout_ref.at[:, half_o], block(wo, r)),
         )
 
     out_swaps = swaps(region, x)
@@ -139,12 +140,14 @@
         wq[pl.ds(pl.multiple_of(region * rows, rows), rows), k * fb : (k + 1) * fb] = wqkv_ref[:, at]
 
     def line(buf, kind, way, s, h, q):
-        ref = block(buf, 2 * q + h)
+        ref = block(buf, 2 * q + h) if kind == 0 else block(buf, q)
         step = 2 if way == 0 else -2
         return remote(
             ref, ref, line_send.at[way, kind, s, h], line_recv.at[way, kind, s, h], region + step, mp
         )
 
+    parts = (2, 1)
+
     def line_do(buf, kind, s, h, act):
         @pl.when(has_down & (plane - s >= 0))
         def _():
@@ -160,12 +163,12 @@
     def line_wait_recv(buf, kind, s):
         @pl.when(plane - s - 1 >= 0)
         def _():
-            for h in range(2):
+            for h in range(parts[kind]):
                 line(buf, kind, 0, s, h, plane - s - 1).wait_recv()
 
         @pl.when(plane + s + 1 <= planes - 1)
         def _():
-            for h in range(2):
+            for h in range(parts[kind]):
                 line(buf, kind, 1, s, h, plane + s + 1).wait_recv()
 
     def line_forward(buf, kind, s):
@@ -173,11 +176,11 @@
 
         @pl.when(s + 1 < planes - 1)
         def _():
-            for h in range(2):
+            for h in range(parts[kind]):
                 line_send_start(buf, kind, s + 1, h)
 
     line_send_start(wq, 0, 0, x)
-    block(wo, region)[...] = wout_ref[:, half_m]
+    block(wo, plane)[...] = wout_ref[...]
     mods[x, 0:3, :] = mod_ref[0]
     slots[x] = tiles_ref[:, :, half_m]
     in_swaps[0].wait_recv()
@@ -207,11 +210,7 @@
     for c in (sends[2], sends[0], sends[1], sends[3]):
         c.start()
     line_forward(wq, 0, 0)
-    in_swaps[2].wait_recv()
-    in_swaps[3].wait_recv()
-    for h in range(2):
-        line_send_start(wo, 1, 0, h)
-
+    line_send_start(wo, 1, 0, 0)
     line_forward(wq, 0, 1)
     if planes > 3:
         line_forward(wo, 1, 0)
@@ -220,6 +219,7 @@
         c = gather(4 + i, blocks[i], region, mp_core)
         c.start()
         sends.append(c)
+    in_swaps[2].wait_recv()
     for i in range(4):
         gather(3 + i, core_blocks[i], region, mp_core).wait_recv()
 
@@ -258,6 +258,7 @@
     heads = fb // HDIM
 
     def attend(t, _):
+        outs = []
         proj = jnp.dot(hidden[t], wq[...], preferred_element_type=F32).astype(BF16)
         for h in range(heads):
             q = proj[:, h * HDIM : (h + 1) * HDIM]
@@ -267,10 +268,8 @@
             scores = scores * (1.0 / math.sqrt(HDIM))
             e = jnp.exp(scores - jnp.max(scores, axis=-1, keepdims=True))
             p = (e / jnp.sum(e, axis=-1, keepdims=True)).astype(BF16)
-            attended[t, :, h * HDIM : (h + 1) * HDIM] = jnp.dot(
-                p, v, preferred_element_type=F32
-            ).astype(BF16)
-
+            outs.append(jnp.dot(p, v, preferred_element_type=F32).astype(BF16))
+        attended[t, :, half_m] = jnp.concatenate(outs, axis=1)
         return 0
 
     odd = plane % 2
@@ -278,20 +277,27 @@
     def tile_at(i):
         return i * odd + (nslot - 1 - i) * (1 - odd)
 
+    def share_heads(i):
+        ref = attended.at[tile_at(i), :, half_m]
+        return remote(ref, ref, heads_send.at[i], heads_recv.at[i], partner, mp)
+
+    def other_heads(i):
+        ref = attended.at[tile_at(i), :, half_o]
+        return remote(ref, ref, heads_send.at[i], heads_recv.at[i], partner, mp)
+
     def attend_at(i, _):
         attend(tile_at(i), 0)
+        share_heads(i).start()
         return 0
 
     attend_at(0, 0)
     line_forward(wo, 1, planes - 3)
-    lax.fori_loop(1, nslot - 1, attend_at, 0)
+    lax.fori_loop(1, nslot, attend_at, 0)
     line_forward(wo, 1, planes - 2)
 
-    def product(b, t):
-        w = wo[pl.ds(pl.multiple_of(b * fb, fb), fb)]
+    def product(m, t):
+        w = wo[pl.ds(pl.multiple_of(m * fb, fb), fb)]
         return lax.dot_general(attended[t], w, (((1,), (1,)), ((), ())), preferred_element_type=F32)
-
-    dests = ((xo, mp_y), (x, mp_y), (xo, mp), (x, mp))
 
     def core_sum(i):
         t = tile_at(i)
@@ -299,50 +305,70 @@
             part_near.at[t], from_core.at[t], near_send.at[i], near_recv.at[i], region, mp_core
         )
 
-    def far_sum(i, d):
-        dx, dm = dests[d]
-        t = tile_at(i)
-        return remote(
-            part_far.at[d, t],
-            from_far.at[d, t],
-            sum_send.at[d, i],
-            sum_recv.at[d, i],
-            plane * 2 + dx,
-            dm,
-        )
+    def far_sum(i):
+        t = tile_at(i)
+        return remote(part_far.at[t], from_far.at[t], sum_send.at[i], sum_recv.at[i], region, mp_y)
 
     def near(i):
         t = tile_at(i)
-        for d, (dx, dm) in enumerate(dests):
-            part_near[t, d] = product((dm + 1 - 2 * core) * 2 + dx, t).astype(BF16)
+        other_heads(i).wait_recv()
+        part_near[t, 0] = product(3 - mp, t).astype(BF16)
+        part_near[t, 1] = product(mp_core, t).astype(BF16)
         core_sum(i).start()
 
     def far(i):
         t = tile_at(i)
         core_sum(i).wait_recv()
-        for d, (dx, dm) in enumerate(dests[:3]):
-            part_far[d, t] = (product(dm * 2 + dx, t) + from_core[t, d].astype(F32)).astype(BF16)
-            far_sum(i, d).start()
+        part_far[t] = (product(mp_y, t) + from_core[t, 0].astype(F32)).astype(BF16)
+        far_sum(i).start()
 
     near(0)
-    attend(tile_at(nslot - 1), 0)
     for i in range(1, nslot):
         near(i)
         far(i - 1)
     far(nslot - 1)
 
-    at_m = pl.ds(pl.multiple_of(mine * fb, fb), fb)
-    gate_e = mods[0, :, at_m].astype(F32)[2:3]
-    gate_d = mods[1, :, at_m].astype(F32)[2:3]
+    groups = fb // rows
+
+    def pick(lo, hi):
+        if groups == 1:
+            return jnp.where(x == 0, lo, hi)
+        both = jnp.concatenate([lo, hi], axis=1)
+        cols = [both[:, g * rows : (g + 1) * rows] for g in range(2 * groups)]
+        return jnp.concatenate(
+            [jnp.where(x == 0, cols[2 * g], cols[2 * g + 1]) for g in range(groups)], axis=1
+        )
+
+    def merge(own, other):
+        evens = jnp.where(x == 0, own, other)
+        odds = jnp.where(x == 0, other, own)
+        if groups == 1:
+            return jnp.concatenate([evens, odds], axis=1)
+        cols = []
+        for g in range(groups):
+            at = slice(g * rows, (g + 1) * rows)
+            cols += [evens[:, at], odds[:, at]]
+        return jnp.concatenate(cols, axis=1)
+
+    def gate_of(g):
+        lo = pl.ds(pl.multiple_of(mp * 2 * fb, fb), fb)
+        hi = pl.ds(pl.multiple_of(mp * 2 * fb + fb, fb), fb)
+        return pick(mods[g, :, lo].astype(F32), mods[g, :, hi].astype(F32))[2:3]
+
+    gate_e = gate_of(0)
+    gate_d = gate_of(1)
 
     def update(i):
         t = tile_at(i)
-        total = product(mine, t) + from_core[t, 3].astype(F32)
-        for d in range(3):
-            far_sum(i, d).wait_recv()
-            total = total + from_far[d, t].astype(F32)
+        total = product(mp, t) + from_core[t, 1].astype(F32)
+        far_sum(i).wait_recv()
+        total = total + from_far[t].astype(F32)
         gate = jnp.where(t < even, gate_e, gate_d)
-        updated[t] = (feats[mine, t].astype(F32) + gate * total).astype(BF16)
+        if groups == 1:
+            tile = feats[mine, t].astype(F32)
+        else:
+            tile = pick(feats[2 * mp, t].astype(F32), feats[2 * mp + 1, t].astype(F32))
+        updated[t] = (tile + gate * total).astype(BF16)
 
     to_side = remote(
         updated.at[tile_at(0)],
@@ -460,14 +486,20 @@
     downward(nslot - 1)
 
     start = x * even
-    for s in range(nslot):
-        got = finished[jnp.clip(start + s, 0, nslot - 1)]
-        out_ref[s, :, half_m] = jnp.where(s < own_count, got, jnp.zeros_like(got))
+    if groups == 1:
+        for s in range(nslot):
+            got = finished[jnp.clip(start + s, 0, nslot - 1)]
+            out_ref[s, :, half_m] = jnp.where(s < own_count, got, jnp.zeros_like(got))
     for i in range(nslot):
         to_owner(i).wait_recv()
     for s in range(nslot):
         got = partner_done[jnp.clip(start + s, 0, nslot - 1)]
-        out_ref[s, :, half_o] = jnp.where(s < own_count, got, jnp.zeros_like(got))
+        if groups == 1:
+            out_ref[s, :, half_o] = jnp.where(s < own_count, got, jnp.zeros_like(got))
+        else:
+            own = finished[jnp.clip(start + s, 0, nslot - 1)]
+            got = merge(own.astype(F32), got.astype(F32)).astype(BF16)
+            out_ref[s] = jnp.where(s < own_count, got, jnp.zeros_like(got))
 
     to_side.wait_send()
     for c in out_swaps:
@@ -477,12 +509,12 @@
     for i in range(nslot):
         to_owner(i).wait_send()
         core_sum(i).wait_send()
-        for d in range(3):
-            far_sum(i, d).wait_send()
+        far_sum(i).wait_send()
+        share_heads(i).wait_send()
 
     def drain(s, _):
         for kind, buf in ((0, wq), (1, wo)):
-            for h in range(2):
+            for h in range(parts[kind]):
                 line_do(buf, kind, s, h, lambda c: c.wait_send())
         return 0
 
@@ -511,28 +543,30 @@
             pltpu.VMEM((2, 16, width), BF16),
             pltpu.VMEM((rows, kinds * fb), BF16),
             pltpu.VMEM((width, kinds * fb), BF16),
-            pltpu.VMEM((width, fb), BF16),
+            pltpu.VMEM((planes * rows, wide), BF16),
             pltpu.VMEM((nslot, tok, width), BF16),
+            pltpu.VMEM((nslot, tok, wide), BF16),
+            pltpu.VMEM((nslot, 2, tok, fb), BF16),
             pltpu.VMEM((nslot, tok, fb), BF16),
-            pltpu.VMEM((nslot, 4, tok, fb), BF16),
-            pltpu.VMEM((3, nslot, tok, fb), BF16),
-            pltpu.VMEM((nslot, 4, tok, fb), BF16),
-            pltpu.VMEM((3, nslot, tok, fb), BF16),
+            pltpu.VMEM((nslot, 2, tok, fb), BF16),
+            pltpu.VMEM((nslot, tok, fb), BF16),
             pltpu.VMEM((nslot, tok, fb), BF16),
             pltpu.VMEM((tok, fb), BF16),
             pltpu.VMEM((2, nslot, W * S, fb), BF16),
             pltpu.VMEM((nslot, tok, fb), BF16),
             pltpu.VMEM((nslot, tok, fb), BF16),
-            dma((4,)),
-            dma((4,)),
+            dma((3,)),
+            dma((3,)),
             dma((7,)),
             dma((7,)),
             dma((2, 2, planes - 1, 2)),
             dma((2, 2, planes - 1, 2)),
             dma((nslot,)),
             dma((nslot,)),
-            dma((3, nslot)),
-            dma((3, nslot)),
+            dma((nslot,)),
+            dma((nslot,)),
+            dma((nslot,)),
+            dma((nslot,)),
             dma((1,)),
             dma((1,)),
             dma((2, nslot)),

time: 126 us -> 117 us (0.929)
  Pallas kernels: 121 us -> 112 us
    pallas_call x1, Pallas kernels: 121 us -> 112 us  [on_device(): pl.pallas_call(functools.partial(kernel, regions), out_shape=jax.ShapeDty...]
where the time goes in v3:
time: 117 us
  Pallas kernels  112 us (96%)
  local copies, waits for them, and re-layouts  4.82 us (4%)
    pallas_call x1, Pallas kernels, on_device(): pl.pallas_call(functools.partial(kernel, regions), out_shape=jax.ShapeDty...  112 us
    unnamed x2, local copies, waits for them, and re-layouts  3.66 us

profile of v3, /device:TPU:0, one launch (start us, length us, event | category | flops | bytes accessed | tf_op | source)
XLA Modules:
  0.0 116.7 jit_solution(16256047699305585068)
XLA Ops:
  0.0 1.4 %copy.8 = bf16[256,3,512]{0,2,1:T(8,128)(2,1)S(1)} copy(bf16[256,3,512]{2,0,1:T(8,128)(2,1)} %param.9) | data formatting | bytes 1572864 | tf_op args[3]
  1.4 1.2 copy.9.wqkv_ref
  2.6 111.8 %shard_map.64 = bf16[4,256,512]{2,1,0:T(8,128)(2,1)} custom-call(s32[8]{0:T(128)} %counts_ref.1, f32[6]{0:T(128)} %blend_ref.1, bf16[4,256,512]{2,1,0:T(8,128)(2,1)} %tiles_ref.1, bf16[1,3,2048]{2,1,0:T(4,128)(2,1)} %mod_ref.1, bf16[256,1536]{1,0:T(8,128)(2,1)} %copy.9.wqkv_ref, bf16[256,512]{1,0:T(8,128)(2,1)} %wout_ref.1), custom_call_target="tpu_custom_call" | custom-call | tf_op jit(solution)/shard_map/pallas_call | solution.py:535
  114.4 2.3 %copy.11 = bf16[4,256,512]{2,1,0:T(8,128)(2,1)} copy(bf16[4,256,512]{2,1,0:T(8,128)(2,1)} %shard_map.64) | data formatting | bytes 2097152

commit v4 on v3

--- a/solution.py
+++ b/solution.py
@@ -75,8 +75,7 @@
     mp_y = (1 - yy) * 2 + core
     nslot, tok, wide = tiles_ref.shape
     fb = wide // 2
-    rows = wqkv_ref.shape[0]
-    kinds = wqkv_ref.shape[1] // wide
+    kinds, rows = wqkv_ref.shape[:2]
     down = TCOLS // nslot
     mine = mp * 2 + x
     has_up = plane > 0
@@ -132,12 +131,10 @@
     out_swaps = swaps(region, x)
     in_swaps = swaps(partner, xo)
     for k in range(kinds):
-        at = pl.ds(pl.multiple_of(k * wide + xo * fb, fb), fb)
-        stage[:, k * fb : (k + 1) * fb] = wqkv_ref[:, at]
+        stage[:, k * fb : (k + 1) * fb] = wqkv_ref[k, :, half_o]
     out_swaps[0].start()
     for k in range(kinds):
-        at = pl.ds(pl.multiple_of(k * wide + x * fb, fb), fb)
-        wq[pl.ds(pl.multiple_of(region * rows, rows), rows), k * fb : (k + 1) * fb] = wqkv_ref[:, at]
+        wq[pl.ds(pl.multiple_of(region * rows, rows), rows), k * fb : (k + 1) * fb] = wqkv_ref[k, :, half_m]
 
     def line(buf, kind, way, s, h, q):
         ref = block(buf, 2 * q + h) if kind == 0 else block(buf, q)
@@ -160,24 +157,25 @@
     def line_send_start(buf, kind, s, h):
         line_do(buf, kind, s, h, lambda c: c.start())
 
-    def line_wait_recv(buf, kind, s):
+    def line_forward(buf, kind, s, h):
         @pl.when(plane - s - 1 >= 0)
         def _():
-            for h in range(parts[kind]):
-                line(buf, kind, 0, s, h, plane - s - 1).wait_recv()
+            line(buf, kind, 0, s, h, plane - s - 1).wait_recv()
 
         @pl.when(plane + s + 1 <= planes - 1)
         def _():
-            for h in range(parts[kind]):
-                line(buf, kind, 1, s, h, plane + s + 1).wait_recv()
-
-    def line_forward(buf, kind, s):
-        line_wait_recv(buf, kind, s)
+            line(buf, kind, 1, s, h, plane + s + 1).wait_recv()
 
         @pl.when(s + 1 < planes - 1)
         def _():
-            for h in range(parts[kind]):
-                line_send_start(buf, kind, s + 1, h)
+            line_send_start(buf, kind, s + 1, h)
+
+    def forward_wq(s):
+        line_forward(wq, 0, s, x)
+        line_forward(wq, 0, s, xo)
+
+    def forward_wo(s):
+        line_forward(wo, 1, s, 0)
 
     line_send_start(wq, 0, 0, x)
     block(wo, plane)[...] = wout_ref[...]
@@ -187,6 +185,7 @@
     line_send_start(wq, 0, 0, xo)
     for c in out_swaps[1:]:
         c.start()
+    line_forward(wq, 0, 0, x)
 
     in_swaps[1].wait_recv()
     even = counts_ref[2 * plane]
@@ -209,11 +208,10 @@
     ]
     for c in (sends[2], sends[0], sends[1], sends[3]):
         c.start()
-    line_forward(wq, 0, 0)
+    line_forward(wq, 0, 0, xo)
     line_send_start(wo, 1, 0, 0)
-    line_forward(wq, 0, 1)
-    if planes > 3:
-        line_forward(wo, 1, 0)
+    forward_wq(1)
+    forward_wo(0)
     for i in range(3):
         gather(i, blocks[i], region, mp_core).wait_recv()
         c = gather(4 + i, blocks[i], region, mp_core)
@@ -248,12 +246,13 @@
     lax.fori_loop(0, nslot, normalise, 0)
 
     def more(s, _):
-        line_forward(wo, 1, s - 1)
-        line_forward(wq, 0, s)
+        forward_wq(s)
+        forward_wo(s - 1)
         return 0
 
     lax.fori_loop(2, planes - 2, more, 0)
-    line_forward(wq, 0, planes - 2)
+    forward_wo(planes - 3)
+    forward_wq(planes - 2)
 
     heads = fb // HDIM
 
@@ -290,10 +289,8 @@
         share_heads(i).start()
         return 0
 
-    attend_at(0, 0)
-    line_forward(wo, 1, planes - 3)
-    lax.fori_loop(1, nslot, attend_at, 0)
-    line_forward(wo, 1, planes - 2)
+    lax.fori_loop(0, nslot, attend_at, 0)
+    forward_wo(planes - 2)
 
     def product(m, t):
         w = wo[pl.ds(pl.multiple_of(m * fb, fb), fb)]
@@ -528,7 +525,7 @@
     width = modulation.shape[2]
     nblock = width // fb
     planes = regions // 2
-    wqkv = qkv_weight.reshape(rows, kinds * wide)
+    wqkv = qkv_weight.transpose(1, 0, 2)
     vmem = pl.BlockSpec(memory_space=pltpu.VMEM)
     smem = pl.BlockSpec(memory_space=pltpu.SMEM)
     dma = pltpu.SemaphoreType.DMA

time: 117 us -> 111 us (0.949)
  Pallas kernels: 112 us -> 109 us
  local copies, waits for them, and re-layouts: 4.82 us -> 2.26 us
    pallas_call x1, Pallas kernels: 112 us -> 109 us  [on_device(): pl.pallas_call(functools.partial(kernel, regions), out_shape=jax.ShapeDty...]
    unnamed x2 -> x1, local copies, waits for them, and re-layouts: 3.66 us -> 2.26 us
where the time goes in v4:
time: 111 us
  Pallas kernels  109 us (98%)
  local copies, waits for them, and re-layouts  2.26 us (2%)
    pallas_call x1, Pallas kernels, on_device(): pl.pallas_call(functools.partial(kernel, regions), out_shape=jax.ShapeDty...  109 us
    unnamed x1, local copies, waits for them, and re-layouts  2.26 us

profile of v4, /device:TPU:0, one launch (start us, length us, event | category | flops | bytes accessed | tf_op | source)
XLA Modules:
  0.0 111.3 jit_solution(5222305441931820043)
XLA Ops:
  0.0 109.0 %shard_map.64 = bf16[4,256,512]{2,1,0:T(8,128)(2,1)} custom-call(s32[8]{0:T(128)} %counts_ref.1, f32[6]{0:T(128)} %blend_ref.1, bf16[4,256,512]{2,1,0:T(8,128)(2,1)} %tiles_ref.1, bf16[1,3,2048]{2,1,0:T(4,128)(2,1)} %mod_ref.1, bf16[3,256,512]{2,1,0:T(8,128)(2,1)} %bitcast.1, bf16[256,512]{1,0:T(8,128)(2,1)} %wout_ref.1), custom_call_target="tpu_custom_call" | custom-call | tf_op jit(solution)/shard_map/pallas_call | solution.py:532
  109.0 2.3 %copy.8 = bf16[4,256,512]{2,1,0:T(8,128)(2,1)} copy(bf16[4,256,512]{2,1,0:T(8,128)(2,1)} %shard_map.64) | data formatting | bytes 2097152

commit v5 on v4

--- a/solution.py
+++ b/solution.py
@@ -105,6 +105,13 @@
         + far_up.astype(jnp.int32)
         + far_down.astype(jnp.int32)
     )
+    half_o = pl.ds(pl.multiple_of(xo * fb, fb), fb)
+    half_m = pl.ds(pl.multiple_of(x * fb, fb), fb)
+    for k in range(kinds):
+        at = slice(k * fb, (k + 1) * fb)
+        wq[pl.ds(pl.multiple_of(region * rows, rows), rows), at] = wqkv_ref[k, :, half_m]
+        stage[:, at] = wqkv_ref[k, :, half_o]
+    wo[pl.ds(pl.multiple_of(plane * rows, rows), rows)] = wout_ref[...]
     pl.semaphore_wait(barrier, arrivals)
 
     def remote(src, dst, ssem, rsem, r, m):
@@ -117,9 +124,6 @@
 
     def swap(i, src, dst):
         return remote(src, dst, swap_send.at[i], swap_recv.at[i], partner, mp)
-
-    half_o = pl.ds(pl.multiple_of(xo * fb, fb), fb)
-    half_m = pl.ds(pl.multiple_of(x * fb, fb), fb)
 
     def swaps(r, g):
         return (
@@ -130,11 +134,7 @@
 
     out_swaps = swaps(region, x)
     in_swaps = swaps(partner, xo)
-    for k in range(kinds):
-        stage[:, k * fb : (k + 1) * fb] = wqkv_ref[k, :, half_o]
     out_swaps[0].start()
-    for k in range(kinds):
-        wq[pl.ds(pl.multiple_of(region * rows, rows), rows), k * fb : (k + 1) * fb] = wqkv_ref[k, :, half_m]
 
     def line(buf, kind, way, s, h, q):
         ref = block(buf, 2 * q + h) if kind == 0 else block(buf, q)
@@ -178,7 +178,7 @@
         line_forward(wo, 1, s, 0)
 
     line_send_start(wq, 0, 0, x)
-    block(wo, plane)[...] = wout_ref[...]
+    line_send_start(wo, 1, 0, 0)
     mods[x, 0:3, :] = mod_ref[0]
     slots[x] = tiles_ref[:, :, half_m]
     in_swaps[0].wait_recv()
@@ -209,7 +209,6 @@
     for c in (sends[2], sends[0], sends[1], sends[3]):
         c.start()
     line_forward(wq, 0, 0, xo)
-    line_send_start(wo, 1, 0, 0)
     forward_wq(1)
     forward_wo(0)
     for i in range(3):
@@ -290,40 +289,62 @@
         return 0
 
     lax.fori_loop(0, nslot, attend_at, 0)
-    forward_wo(planes - 2)
 
     def product(m, t):
         w = wo[pl.ds(pl.multiple_of(m * fb, fb), fb)]
         return lax.dot_general(attended[t], w, (((1,), (1,)), ((), ())), preferred_element_type=F32)
 
-    def core_sum(i):
+    def core_sum(i, j):
         t = tile_at(i)
         return remote(
-            part_near.at[t], from_core.at[t], near_send.at[i], near_recv.at[i], region, mp_core
+            part_near.at[t, j],
+            from_core.at[t, j],
+            near_send.at[i, j],
+            near_recv.at[i, j],
+            region,
+            mp_core,
         )
 
     def far_sum(i):
         t = tile_at(i)
         return remote(part_far.at[t], from_far.at[t], sum_send.at[i], sum_recv.at[i], region, mp_y)
 
-    def near(i):
-        t = tile_at(i)
+    def near(i, wanted):
+        t = tile_at(i)
+        for j, m in ((0, 3 - mp), (1, mp_core)):
+
+            @pl.when(wanted(m))
+            def _(j=j, m=m):
+                part_near[t, j] = product(m, t).astype(BF16)
+                core_sum(i, j).start()
+
+    def far(i, wanted):
+        t = tile_at(i)
+
+        @pl.when(wanted(mp_y))
+        def _():
+            core_sum(i, 0).wait_recv()
+            part_far[t] = (product(mp_y, t) + from_core[t, 0].astype(F32)).astype(BF16)
+            far_sum(i).start()
+
+    latest = jnp.where(plane < planes // 2, 3, 0)
+
+    def early(m):
+        return m != latest
+
+    def late(m):
+        return m == latest
+
+    for i in range(nslot):
         other_heads(i).wait_recv()
-        part_near[t, 0] = product(3 - mp, t).astype(BF16)
-        part_near[t, 1] = product(mp_core, t).astype(BF16)
-        core_sum(i).start()
-
-    def far(i):
-        t = tile_at(i)
-        core_sum(i).wait_recv()
-        part_far[t] = (product(mp_y, t) + from_core[t, 0].astype(F32)).astype(BF16)
-        far_sum(i).start()
-
-    near(0)
-    for i in range(1, nslot):
-        near(i)
-        far(i - 1)
-    far(nslot - 1)
+        near(i, early)
+        if i > 0:
+            far(i - 1, early)
+    far(nslot - 1, early)
+    forward_wo(planes - 2)
+    for i in range(nslot):
+        near(i, late)
+        far(i, late)
 
     groups = fb // rows
 
@@ -357,7 +378,9 @@
 
     def update(i):
         t = tile_at(i)
-        total = product(mp, t) + from_core[t, 1].astype(F32)
+        total = product(mp, t)
+        core_sum(i, 1).wait_recv()
+        total = total + from_core[t, 1].astype(F32)
         far_sum(i).wait_recv()
         total = total + from_far[t].astype(F32)
         gate = jnp.where(t < even, gate_e, gate_d)
@@ -505,7 +528,8 @@
         c.wait_send()
     for i in range(nslot):
         to_owner(i).wait_send()
-        core_sum(i).wait_send()
+        core_sum(i, 0).wait_send()
+        core_sum(i, 1).wait_send()
         far_sum(i).wait_send()
         share_heads(i).wait_send()
 
@@ -560,8 +584,8 @@
             dma((2, 2, planes - 1, 2)),
             dma((nslot,)),
             dma((nslot,)),
-            dma((nslot,)),
-            dma((nslot,)),
+            dma((nslot, 2)),
+            dma((nslot, 2)),
             dma((nslot,)),
             dma((nslot,)),
             dma((1,)),

time: 111 us -> 113 us (1.018)
    pallas_call x1, Pallas kernels: 109 us -> 110 us  [on_device(): pl.pallas_call(functools.partial(kernel, regions), out_shape=jax.ShapeDty...]
where the time goes in v5:
time: 113 us
  Pallas kernels  110 us (97%)
  local copies, waits for them, and re-layouts  2.26 us (2%)
    pallas_call x1, Pallas kernels, on_device(): pl.pallas_call(functools.partial(kernel, regions), out_shape=jax.ShapeDty...  110 us
    unnamed x1, local copies, waits for them, and re-layouts  2.26 us

profile of v5, /device:TPU:0, one launch (start us, length us, event | category | flops | bytes accessed | tf_op | source)
XLA Modules:
  0.0 112.6 jit_solution(7469791732431815750)
XLA Ops:
  0.0 110.3 %shard_map.64 = bf16[4,256,512]{2,1,0:T(8,128)(2,1)} custom-call(s32[8]{0:T(128)} %counts_ref.1, f32[6]{0:T(128)} %blend_ref.1, bf16[4,256,512]{2,1,0:T(8,128)(2,1)} %tiles_ref.1, bf16[1,3,2048]{2,1,0:T(4,128)(2,1)} %mod_ref.1, bf16[3,256,512]{2,1,0:T(8,128)(2,1)} %bitcast.1, bf16[256,512]{1,0:T(8,128)(2,1)} %wout_ref.1), custom_call_target="tpu_custom_call" | custom-call | tf_op jit(solution)/shard_map/pallas_call | solution.py:556
  110.3 2.3 %copy.8 = bf16[4,256,512]{2,1,0:T(8,128)(2,1)} copy(bf16[4,256,512]{2,1,0:T(8,128)(2,1)} %shard_map.64) | data formatting | bytes 2097152

commit v6 on v5

--- a/solution.py
+++ b/solution.py
@@ -178,7 +178,6 @@
         line_forward(wo, 1, s, 0)
 
     line_send_start(wq, 0, 0, x)
-    line_send_start(wo, 1, 0, 0)
     mods[x, 0:3, :] = mod_ref[0]
     slots[x] = tiles_ref[:, :, half_m]
     in_swaps[0].wait_recv()
@@ -198,24 +197,41 @@
     def gather(i, b, r, m):
         return remote(feats.at[b], feats.at[b], gather_send.at[i], gather_recv.at[i], r, m)
 
-    blocks = (mp * 2 + xo, mp_y * 2 + x, mp_y * 2 + xo)
+    from_x, from_y, diagonal = mp * 2 + xo, mp_y * 2 + x, mp_y * 2 + xo
     core_blocks = (mp_core * 2 + x, mp_core * 2 + xo, (3 - mp) * 2 + x, (3 - mp) * 2 + xo)
+    half = nslot // 2
+
+    def gather_half(i, b, r, m):
+        ref = feats.at[b, pl.ds(i * half, half)]
+        return remote(ref, ref, gather_send.at[7 + i], gather_recv.at[7 + i], r, m)
+
     sends = [
         gather(0, mine, partner, mp),
         gather(1, mine, region, mp_y),
-        gather(2, mine, partner, mp_y),
         gather(3, mine, region, mp_core),
     ]
-    for c in (sends[2], sends[0], sends[1], sends[3]):
+    for c in sends:
         c.start()
     line_forward(wq, 0, 0, xo)
-    forward_wq(1)
-    forward_wo(0)
-    for i in range(3):
-        gather(i, blocks[i], region, mp_core).wait_recv()
-        c = gather(4 + i, blocks[i], region, mp_core)
+    line_forward(wq, 0, 1, x)
+    gather(0, from_x, partner, mp).wait_recv()
+    gather(1, from_y, region, mp_y).wait_recv()
+    passed = [
+        gather_half(0, from_y, partner, mp),
+        gather_half(1, from_x, region, mp_y),
+        gather(4, from_x, region, mp_core),
+        gather(5, from_y, region, mp_core),
+    ]
+    for c in passed:
         c.start()
-        sends.append(c)
+    sends += passed
+    line_forward(wq, 0, 1, xo)
+    gather_half(0, diagonal, partner, mp).wait_recv()
+    gather_half(1, diagonal, region, mp_y).wait_recv()
+    c = gather(6, diagonal, region, mp_core)
+    c.start()
+    sends.append(c)
+    line_send_start(wo, 1, 0, 0)
     in_swaps[2].wait_recv()
     for i in range(4):
         gather(3 + i, core_blocks[i], region, mp_core).wait_recv()
@@ -246,11 +262,10 @@
 
     def more(s, _):
         forward_wq(s)
-        forward_wo(s - 1)
+        forward_wo(s - 2)
         return 0
 
     lax.fori_loop(2, planes - 2, more, 0)
-    forward_wo(planes - 3)
     forward_wq(planes - 2)
 
     heads = fb // HDIM
@@ -288,7 +303,11 @@
         share_heads(i).start()
         return 0
 
-    lax.fori_loop(0, nslot, attend_at, 0)
+    attend_at(0, 0)
+    forward_wo(planes - 4)
+    attend_at(1, 0)
+    forward_wo(planes - 3)
+    lax.fori_loop(2, nslot, attend_at, 0)
 
     def product(m, t):
         w = wo[pl.ds(pl.multiple_of(m * fb, fb), fb)]
@@ -578,8 +597,8 @@
             pltpu.VMEM((nslot, tok, fb), BF16),
             dma((3,)),
             dma((3,)),
-            dma((7,)),
-            dma((7,)),
+            dma((9,)),
+            dma((9,)),
             dma((2, 2, planes - 1, 2)),
             dma((2, 2, planes - 1, 2)),
             dma((nslot,)),

time: 113 us -> 111 us (0.982)
    pallas_call x1, Pallas kernels: 110 us -> 109 us  [on_device(): pl.pallas_call(functools.partial(kernel, regions), out_shape=jax.ShapeDty...]
where the time goes in v6:
time: 111 us
  Pallas kernels  109 us (98%)
  local copies, waits for them, and re-layouts  2.26 us (2%)
    pallas_call x1, Pallas kernels, on_device(): pl.pallas_call(functools.partial(kernel, regions), out_shape=jax.ShapeDty...  109 us
    unnamed x1, local copies, waits for them, and re-layouts  2.26 us

profile of v6, /device:TPU:0, one launch (start us, length us, event | category | flops | bytes accessed | tf_op | source)
XLA Modules:
  0.0 111.2 jit_solution(10607398128289341893)
XLA Ops:
  0.0 108.9 %shard_map.64 = bf16[4,256,512]{2,1,0:T(8,128)(2,1)} custom-call(s32[8]{0:T(128)} %counts_ref.1, f32[6]{0:T(128)} %blend_ref.1, bf16[4,256,512]{2,1,0:T(8,128)(2,1)} %tiles_ref.1, bf16[1,3,2048]{2,1,0:T(4,128)(2,1)} %mod_ref.1, bf16[3,256,512]{2,1,0:T(8,128)(2,1)} %bitcast.1, bf16[256,512]{1,0:T(8,128)(2,1)} %wout_ref.1), custom_call_target="tpu_custom_call" | custom-call | tf_op jit(solution)/shard_map/pallas_call | solution.py:575
  108.9 2.3 %copy.8 = bf16[4,256,512]{2,1,0:T(8,128)(2,1)} copy(bf16[4,256,512]{2,1,0:T(8,128)(2,1)} %shard_map.64) | data formatting | bytes 2097152

commit v7 on v6

--- a/solution.py
+++ b/solution.py
@@ -33,6 +33,7 @@
     wq,
     wo,
     hidden,
+    partial,
     attended,
     part_near,
     part_far,
@@ -238,27 +239,44 @@
 
     nblock = feats.shape[0]
     inv = 1.0 / (nblock * fb)
-    mod_e = mods[0].astype(F32)
-    mod_d = mods[1].astype(F32)
-
-    def normalise(t, _):
-        total = jnp.zeros((tok, 1), F32)
+    shift_e, gain_e = mods[0].astype(F32)[0:1], 1.0 + mods[0].astype(F32)[1:2]
+    shift_d, gain_d = mods[1].astype(F32)[0:1], 1.0 + mods[1].astype(F32)[1:2]
+    lines = 64
+    chunks = tok // lines
+
+    def normalise(i, _):
+        t = i // chunks
+        at_rows = pl.ds(pl.multiple_of((i % chunks) * lines, lines), lines)
+        total = feats[0, t, at_rows].astype(F32)
+        for b in range(1, nblock):
+            total = total + feats[b, t, at_rows].astype(F32)
+        mean = jnp.sum(total, axis=1, keepdims=True) * inv
+        total = jnp.zeros((lines, fb), F32)
         for b in range(nblock):
-            total = total + jnp.sum(feats[b, t].astype(F32), axis=1, keepdims=True)
-        mean = total * inv
-        total = jnp.zeros((tok, 1), F32)
-        for b in range(nblock):
-            c = feats[b, t].astype(F32) - mean
-            total = total + jnp.sum(c * c, axis=1, keepdims=True)
-        scale = lax.rsqrt(total * inv + 1e-06)
-        mod = jnp.where(t < even, mod_e, mod_d)
+            c = feats[b, t, at_rows].astype(F32) - mean
+            total = total + c * c
+        scale = lax.rsqrt(jnp.sum(total, axis=1, keepdims=True) * inv + 1e-06)
+        shift = jnp.where(t < even, shift_e, shift_d)
+        gain = jnp.where(t < even, gain_e, gain_d)
         for b in range(nblock):
             at = slice(b * fb, (b + 1) * fb)
-            c = (feats[b, t].astype(F32) - mean) * scale
-            hidden[t, :, at] = (c * (1.0 + mod[1:2, at]) + mod[0:1, at]).astype(BF16)
+            c = (feats[b, t, at_rows].astype(F32) - mean) * scale
+            hidden[t, at_rows, at] = (c * gain[:, at] + shift[:, at]).astype(BF16)
         return 0
 
-    lax.fori_loop(0, nslot, normalise, 0)
+    lax.fori_loop(0, nslot * chunks, normalise, 0)
+
+    latest = jnp.where(plane < planes // 2, 3, 0)
+    group = feats.shape[0] * fb // 4
+
+    def multiply(t, g):
+        at = pl.ds(pl.multiple_of(g * group, group), group)
+        return jnp.dot(hidden[t, :, at], wq[at], preferred_element_type=F32)
+
+    def begin(t, _):
+        total = multiply(t, (latest + 1) % 4) + multiply(t, (latest + 2) % 4)
+        partial[t] = total + multiply(t, (latest + 3) % 4)
+        return 0
 
     def more(s, _):
         forward_wq(s)
@@ -266,21 +284,21 @@
         return 0
 
     lax.fori_loop(2, planes - 2, more, 0)
+    lax.fori_loop(0, nslot, begin, 0)
     forward_wq(planes - 2)
 
     heads = fb // HDIM
 
     def attend(t, _):
         outs = []
-        proj = jnp.dot(hidden[t], wq[...], preferred_element_type=F32).astype(BF16)
+        proj = (partial[t] + multiply(t, latest)).astype(BF16)
         for h in range(heads):
             q = proj[:, h * HDIM : (h + 1) * HDIM]
             k = proj[:, fb + h * HDIM : fb + (h + 1) * HDIM]
             v = proj[:, 2 * fb + h * HDIM : 2 * fb + (h + 1) * HDIM]
             scores = lax.dot_general(q, k, (((1,), (1,)), ((), ())), preferred_element_type=F32)
-            scores = scores * (1.0 / math.sqrt(HDIM))
-            e = jnp.exp(scores - jnp.max(scores, axis=-1, keepdims=True))
-            p = (e / jnp.sum(e, axis=-1, keepdims=True)).astype(BF16)
+            e = jnp.exp((scores - jnp.max(scores, axis=-1, keepdims=True)) * (1.0 / math.sqrt(HDIM)))
+            p = (e * (1.0 / jnp.sum(e, axis=-1, keepdims=True))).astype(BF16)
             outs.append(jnp.dot(p, v, preferred_element_type=F32).astype(BF16))
         attended[t, :, half_m] = jnp.concatenate(outs, axis=1)
         return 0
@@ -345,8 +363,6 @@
             core_sum(i, 0).wait_recv()
             part_far[t] = (product(mp_y, t) + from_core[t, 0].astype(F32)).astype(BF16)
             far_sum(i).start()
-
-    latest = jnp.where(plane < planes // 2, 3, 0)
 
     def early(m):
         return m != latest
@@ -585,6 +601,7 @@
             pltpu.VMEM((width, kinds * fb), BF16),
             pltpu.VMEM((planes * rows, wide), BF16),
             pltpu.VMEM((nslot, tok, width), BF16),
+            pltpu.VMEM((nslot, tok, kinds * fb), F32),
             pltpu.VMEM((nslot, tok, wide), BF16),
             pltpu.VMEM((nslot, 2, tok, fb), BF16),
             pltpu.VMEM((nslot, tok, fb), BF16),

time: 111 us -> 107 us (0.964)
  Pallas kernels: 109 us -> 105 us
    pallas_call x1, Pallas kernels: 109 us -> 105 us  [on_device(): pl.pallas_call(functools.partial(kernel, regions), out_shape=jax.ShapeDty...]
where the time goes in v7:
time: 107 us
  Pallas kernels  105 us (98%)
  local copies, waits for them, and re-layouts  2.26 us (2%)
    pallas_call x1, Pallas kernels, on_device(): pl.pallas_call(functools.partial(kernel, regions), out_shape=jax.ShapeDty...  105 us
    unnamed x1, local copies, waits for them, and re-layouts  2.26 us

profile of v7, /device:TPU:0, one launch (start us, length us, event | category | flops | bytes accessed | tf_op | source)
XLA Modules:
  0.0 107.1 jit_solution(6609975245734612306)
XLA Ops:
  0.0 104.9 %shard_map.64 = bf16[4,256,512]{2,1,0:T(8,128)(2,1)} custom-call(s32[8]{0:T(128)} %counts_ref.1, f32[6]{0:T(128)} %blend_ref.1, bf16[4,256,512]{2,1,0:T(8,128)(2,1)} %tiles_ref.1, bf16[1,3,2048]{2,1,0:T(4,128)(2,1)} %mod_ref.1, bf16[3,256,512]{2,1,0:T(8,128)(2,1)} %bitcast.1, bf16[256,512]{1,0:T(8,128)(2,1)} %wout_ref.1), custom_call_target="tpu_custom_call" | custom-call | tf_op jit(solution)/shard_map/pallas_call | solution.py:591
  104.9 2.3 %copy.8 = bf16[4,256,512]{2,1,0:T(8,128)(2,1)} copy(bf16[4,256,512]{2,1,0:T(8,128)(2,1)} %shard_map.64) | data formatting | bytes 2097152

commit v8 on v7

--- a/solution.py
+++ b/solution.py
@@ -227,12 +227,12 @@
         c.start()
     sends += passed
     line_forward(wq, 0, 1, xo)
+    line_send_start(wo, 1, 0, 0)
     gather_half(0, diagonal, partner, mp).wait_recv()
     gather_half(1, diagonal, region, mp_y).wait_recv()
     c = gather(6, diagonal, region, mp_core)
     c.start()
     sends.append(c)
-    line_send_start(wo, 1, 0, 0)
     in_swaps[2].wait_recv()
     for i in range(4):
         gather(3 + i, core_blocks[i], region, mp_core).wait_recv()
@@ -323,9 +323,9 @@
 
     attend_at(0, 0)
     forward_wo(planes - 4)
-    attend_at(1, 0)
+    lax.fori_loop(1, nslot - 1, attend_at, 0)
     forward_wo(planes - 3)
-    lax.fori_loop(2, nslot, attend_at, 0)
+    attend_at(nslot - 1, 0)
 
     def product(m, t):
         w = wo[pl.ds(pl.multiple_of(m * fb, fb), fb)]

time: 107 us -> 109 us (1.019)
    pallas_call x1, Pallas kernels: 105 us -> 106 us  [on_device(): pl.pallas_call(functools.partial(kernel, regions), out_shape=jax.ShapeDty...]
where the time goes in v8:
time: 109 us
  Pallas kernels  106 us (97%)
  local copies, waits for them, and re-layouts  2.26 us (2%)
    pallas_call x1, Pallas kernels, on_device(): pl.pallas_call(functools.partial(kernel, regions), out_shape=jax.ShapeDty...  106 us
    unnamed x1, local copies, waits for them, and re-layouts  2.26 us

profile of v8, /device:TPU:0, one launch (start us, length us, event | category | flops | bytes accessed | tf_op | source)
XLA Modules:
  0.0 108.6 jit_solution(3477191902058035786)
XLA Ops:
  0.0 106.3 %shard_map.64 = bf16[4,256,512]{2,1,0:T(8,128)(2,1)} custom-call(s32[8]{0:T(128)} %counts_ref.1, f32[6]{0:T(128)} %blend_ref.1, bf16[4,256,512]{2,1,0:T(8,128)(2,1)} %tiles_ref.1, bf16[1,3,2048]{2,1,0:T(4,128)(2,1)} %mod_ref.1, bf16[3,256,512]{2,1,0:T(8,128)(2,1)} %bitcast.1, bf16[256,512]{1,0:T(8,128)(2,1)} %wout_ref.1), custom_call_target="tpu_custom_call" | custom-call | tf_op jit(solution)/shard_map/pallas_call | solution.py:591
  106.4 2.3 %copy.8 = bf16[4,256,512]{2,1,0:T(8,128)(2,1)} copy(bf16[4,256,512]{2,1,0:T(8,128)(2,1)} %shard_map.64) | data formatting | bytes 2097152
